TPU v7x, 256 devices: a whole 4x4x8 slice. The times are simulated.
256 devices in a mesh: seq: 32 (over y, z_lo, core), tp: 8 (over x, z_hi).
Axes of the slice: x: 4, y: 4, z: 8 (z_hi: 2, z_lo: 4; z = z_hi * 4 + z_lo), core: 2. Of those that a mesh axis runs over, the one named last changes fastest.
Arguments:
- hidden_in: bfloat16 [16384, 4096], P(('seq', 'tp')), may hold values from -10 to 10
- norm_gain: float32 [4096], replicated, may hold values from 0.1 to 1.9
- qkv_weight: bfloat16 [4096, 3, 2048], P(None, None, 'tp'), may hold values from -1 to 1
- out_weight: bfloat16 [2048, 4096], P('tp'), may hold values from -0.125 to 0.125
- block_order: int32 [128], replicated, may hold values from 0 to 127, each once
Outputs:
- attended: bfloat16 [16384, 4096], P(('seq', 'tp'))
Inputs may be any that keep to these rules, and one draw needn't show every extreme that they name: `block_order`: each sequence block appears exactly once.
All inputs are finite; a program needn't handle non-finite values.
Results may differ from a plain program's by a relative error of at most 0.019.
Values may be sent and summed in bfloat16 or wider, within the bound.
A program may use at most 128 MiB of HBM per device.

v0:
```python
import math

import jax
import jax.numpy as jnp
from jax import lax
from jax.sharding import PartitionSpec as P

HD = 128
BLK = 128


def rotate(tensor, position):
    half = tensor.shape[-1] // 2
    inv_freq = 10000.0 ** (-(jnp.arange(half, dtype=jnp.float32) * 2.0 / tensor.shape[-1]))
    angle = position.astype(jnp.float32)[:, None] * inv_freq[None, :]
    cosine = jnp.cos(angle)[:, None, :]
    sine = jnp.sin(angle)[:, None, :]
    first = tensor[..., :half]
    second = tensor[..., half:]
    return jnp.concatenate(
        [first * cosine - second * sine, second * cosine + first * sine], axis=-1
    )


def attend_tile(carry, queries, qpos, keys, values, kpos, factor):
    top, total, summed = carry
    keep = kpos[None, :] <= qpos[:, None]

    def work(state):
        old_top, old_total, old_sum = state
        score = (
            jnp.einsum("qhd,khd->hqk", queries, keys, preferred_element_type=jnp.float32) * factor
        )
        score = jnp.where(keep[None], score, -1e30)
        new_top = jnp.maximum(old_top, jnp.max(score, axis=-1))
        shrink = jnp.exp(old_top - new_top)
        weight = jnp.where(keep[None], jnp.exp(score - new_top[..., None]), 0.0)
        new_total = old_total * shrink + jnp.sum(weight, axis=-1)
        new_sum = old_sum * shrink[..., None] + jnp.einsum(
            "hqk,khd->hqd", weight.astype(jnp.bfloat16), values, preferred_element_type=jnp.float32
        )
        return (new_top, new_total, new_sum)

    return lax.cond(jnp.min(kpos) <= jnp.max(qpos), work, lambda state: state, (top, total, summed))


def local(hidden_in, norm_gain, qkv_weight, out_weight, block_order):
    heads_dev = qkv_weight.shape[2] // HD
    local_rows = hidden_in.shape[0]
    tok_rows = local_rows * lax.axis_size("tp")
    factor = 1.0 / HD**0.5
    position = (block_order[:, None] * BLK + jnp.arange(BLK, dtype=jnp.int32)[None, :]).reshape(-1)
    floats = hidden_in.astype(jnp.float32)
    scale_row = lax.rsqrt(jnp.mean(floats * floats, axis=-1, keepdims=True) + 1e-05)
    normed = (floats * scale_row * norm_gain[None, :]).astype(jnp.bfloat16)
    weight_flat = qkv_weight.reshape(qkv_weight.shape[0], 3 * heads_dev * HD)
    gathered = lax.all_gather(normed, "tp", axis=0, tiled=True)
    projected = jnp.dot(gathered, weight_flat, preferred_element_type=jnp.float32)
    projected = projected.reshape(tok_rows, 3, heads_dev, HD)
    my_start = lax.axis_index("seq") * tok_rows
    qpos = lax.dynamic_slice_in_dim(position, my_start, tok_rows, 0)
    rot_query = rotate(projected[:, 0], qpos).astype(jnp.bfloat16)
    rot_key = rotate(projected[:, 1], qpos).astype(jnp.bfloat16)
    value = projected[:, 2].astype(jnp.bfloat16)
    init = (
        jnp.full((heads_dev, tok_rows), -1e30, jnp.float32),
        jnp.zeros((heads_dev, tok_rows), jnp.float32),
        jnp.zeros((heads_dev, tok_rows, HD), jnp.float32),
    )
    keys = lax.all_gather(rot_key, "seq", axis=0, tiled=True)
    values = lax.all_gather(value, "seq", axis=0, tiled=True)
    count = keys.shape[0]
    tile = math.gcd(count, 512)
    stacked = (
        keys.reshape(count // tile, tile, heads_dev, HD),
        values.reshape(count // tile, tile, heads_dev, HD),
        position.reshape(count // tile, tile),
    )

    def step(state, item):
        return (attend_tile(state, rot_query, qpos, item[0], item[1], item[2], factor), None)

    result, unused = lax.scan(step, init, stacked)
    top, total, summed = result
    context = summed / total[..., None]
    context = jnp.transpose(context.astype(jnp.bfloat16), (1, 0, 2)).reshape(
        tok_rows, heads_dev * HD
    )
    term = jnp.dot(context, out_weight, preferred_element_type=jnp.float32)
    attended = lax.psum_scatter(term.astype(jnp.bfloat16), "tp", scatter_dimension=0, tiled=True)
    return attended


def solution(mesh):
    in_specs = (P(("seq", "tp"), None), P(), P(None, None, "tp"), P("tp", None), P())
    out_specs = P(("seq", "tp"), None)
    return jax.shard_map(local, mesh=mesh, in_specs=in_specs, out_specs=out_specs, check_vma=False)
```

profile of v0, /device:TPU:33, one launch (start us, length us, event | category | flops | bytes accessed | tf_op | source)
XLA Modules:
  0.0 625.6 jit_solution(1737732550482689104)
XLA Ops:
  10.1 8.8 %copy.11 = bf16[4096,3,256]{0,2,1:T(8,128)(2,1)} copy(bf16[4096,3,256]{2,0,1:T(8,128)(2,1)} %param.11) | data formatting | bytes 12582912 | tf_op args[2]
  19.6 98.9 %all-gather.5.cloned.1.call-done = bf16[512,4096]{1,0:T(8,128)(2,1)} async-done(((bf16[64,4096]{1,0:T(8,128)(2,1)}), bf16[512,4096]{1,0:T(8,128)(2,1)}) %all-gather.5.cloned.1.call-update) | async-done | bytes 4194320 | tf_op jit(solution)/shard_map/all_gather | solution.py:57
  118.5 6.8 %fusion.18 = f32[512,3,2,128]{0,3,2,1:T(8,128)S(1)} fusion(bf16[3,2,128,4096]{3,2,1,0:T(8,128)(2,1)} %bitcast.65, bf16[512,4096]{1,0:T(8,128)(2,1)} %all-gather.5.cloned.1.call-done), kind=kOutput, calls=%fused_computation.25 | convolution fusion | flops 3221225472 | bytes 12058624 | tf_op jit(solution)/shard_map/dot_general | solution.py:58
  130.3 62.4 %all-gather.7.cloned.1.call-done = bf16[16384,2,128]{0,2,1:T(8,128)(2,1)} async-done(((bf16[512,2,128]{0,2,1:T(8,128)(2,1)}), bf16[16384,2,128]{0,2,1:T(8,128)(2,1)}) %all-gather.7.cloned.1.call-update) | async-done | bytes 8388624 | tf_op jit(solution)/shard_map/all_gather | solution.py:70
  192.8 10.4 %copy.19 = bf16[32,8,32,512]{3,2,1,0:T(8,128)(2,1)} copy(bf16[32,8,32,512]{3,1,2,0:T(8,128)(2,1)} %bitcast.63) | data formatting | bytes 16777216
  203.2 14.8 %copy.12 = bf16[32,512,2,128]{3,1,2,0:T(8,128)(2,1)} copy(bf16[32,512,2,128]{1,0,3,2:T(8,128)(2,1)} %bitcast.61) | data formatting | bytes 16777216 | tf_op jit(solution)/shard_map/while | solution.py:83
  218.0 44.5 %all-gather.9.cloned.1.call-done = bf16[16384,1,2,128]{0,3,2,1:T(8,128)(2,1)} async-done(((bf16[512,1,2,128]{0,3,2,1:T(8,128)(2,1)}), bf16[16384,1,2,128]{0,3,2,1:T(8,128)(2,1)}) %all-gather.9.cloned.1.call-update) | async-done | bytes 8388624 | tf_op jit(solution)/shard_map/all_gather | solution.py:71
  262.4 10.4 %copy.20 = bf16[32,8,32,512]{3,2,1,0:T(8,128)(2,1)} copy(bf16[32,8,32,512]{3,1,2,0:T(8,128)(2,1)} %bitcast.64) | data formatting | bytes 16777216
  272.9 14.6 %copy.14 = bf16[32,512,2,128]{3,1,2,0:T(8,128)(2,1)} copy(bf16[32,512,2,128]{1,0,3,2:T(8,128)(2,1)} %bitcast.62) | data formatting | bytes 16777216 | tf_op jit(solution)/shard_map/while | solution.py:83
  287.5 204.5 %while.15 = (s32[]{:T(128)}, f32[2,512]{1,0:T(2,128)S(1)}, f32[2,512]{1,0:T(2,128)S(1)}, f32[2,512,128]{2,1,0:T(8,128)S(1)}, s32[32,512]{1,0:T(8,128)S(1)}, /*in...) while((s32[]{:T(128)}, f32[2,512]{1,0:T(2,128)S(1)}, ...), condition=%wide.region_8.9_spmd, body=%wide.region_2.8_spmd.sunk | while | flops 275778048 | bytes 9250051 | solution.py:83
  289.5 4.4 conditional.2
  295.9 4.4 conditional.2
  302.3 4.4 conditional.2
  308.7 4.4 conditional.2
  315.1 4.4 conditional.2
  321.5 4.4 conditional.2
  327.9 4.4 conditional.2
  334.3 4.4 conditional.2
  340.7 4.4 conditional.2
  347.1 4.4 conditional.2
  353.5 4.4 conditional.2
  359.9 4.4 conditional.2
  366.2 4.4 conditional.2
  372.6 4.4 conditional.2
  379.0 4.4 conditional.2
  385.4 4.4 conditional.2
  391.8 4.4 conditional.2
  398.2 4.4 conditional.2
  455.7 4.4 conditional.2
  462.1 4.4 conditional.2
  468.5 4.4 conditional.2
  495.6 123.5 %reduce-scatter.2.cloned.1.call-done = bf16[64,4096]{1,0:T(8,128)(2,1)} async-done(((bf16[512,4096]{1,0:T(8,128)(2,1)}), bf16[64,4096]{1,0:T(8,128)(2,1)}) %reduce-scatter.2.cloned.1.call-update) | async-done | bytes 524304 | tf_op jit(solution)/shard_map/reduce_scatter | solution.py:90
  (306 shorter events, 220.1 us)
Async XLA Ops:
  6.5 485.8 %copy-start = (bf16[256,4096]{1,0:T(8,128)(2,1)S(1)}, bf16[256,4096]{1,0:T(8,128)(2,1)}, u32[]{:S(2)}) copy-start(bf16[256,4096]{1,0:T(8,128)(2,1)} %param.12) | copy-start | bytes 6291460
  6.5 112.0 %all-gather.5.cloned.1.call-start = ((), (), s32[]{:S(2)}) async-start(), calls=%async_computation.1 | async-start | bytes 4718592 | tf_op jit(solution)/shard_map/all_gather | solution.py:57
  10.0 182.8 %all-gather.7.cloned.1.call-start = ((), (), s32[]{:S(2)}) async-start(), calls=%async_computation.2 | async-start | bytes 8650752 | tf_op jit(solution)/shard_map/all_gather | solution.py:70
  10.1 8.9 %copy-start.2 = (s32[128]{0:T(128)S(1)}, s32[128]{0:T(128)}, u32[]{:S(2)}) copy-start(s32[128]{0:T(128)} %param.13) | copy-start | bytes 1540
  125.3 1.2 copy-start.1
  127.3 135.2 %all-gather.9.cloned.1.call-start = ((), (), s32[]{:S(2)}) async-start(), calls=%async_computation.4 | async-start | bytes 8650752 | tf_op jit(solution)/shard_map/all_gather | solution.py:71
  129.2 489.9 %reduce-scatter.2.cloned.1.call-start = ((), (), s32[]{:S(2)}) async-start(), calls=%async_computation.3 | async-start | bytes 4718592 | tf_op jit(solution)/shard_map/reduce_scatter | solution.py:90
Sparse Core Ops, SparseCore 0:
  10.1 108.3 all-gather.4
  127.4 65.3 all-gather.6
  194.6 67.7 all-gather.8
  495.7 123.2 reduce-scatter.1
where the time goes:
time: 631 us; the launch traced here: 626 us
  waiting for transfers between devices  329 us (52%)
  matrix products  123 us (19%)
  local copies, waits for them, and re-layouts  62.5 us (10%)
  other arithmetic  52 us (8%)
  loops' own time  45.3 us (7%)
  between operations  13.3 us (2%)
    reduce_scatter x1, waiting for transfers between devices, local(): lax.psum_scatter(term.astype(jnp.bfloat16), 'tp', scatter_dimension=0, ti...  123 us
    all_gather x1, waiting for transfers between devices, local(): gathered = lax.all_gather(normed, 'tp', axis=0, tiled=True)  98.9 us
    dot_general x32, matrix products, work(): jnp.einsum('hqk,khd->hqd', weight.astype(jnp.bfloat16), values, preferred...  64.9 us
    all_gather x1, waiting for transfers between devices, local(): keys = lax.all_gather(rot_key, 'seq', axis=0, tiled=True)  62.4 us
    dot_general x32, matrix products, work(): jnp.einsum('qhd,khd->hqk', queries, keys, preferred_element_type=jnp.floa...  48.1 us
    all_gather x1, waiting for transfers between devices, local(): values = lax.all_gather(value, 'seq', axis=0, tiled=True)  44.5 us
    another operation x1, loops' own time, local(): result, unused = lax.scan(step, init, stacked)  43.7 us
    unnamed x9, local copies, waits for them, and re-layouts  30.6 us
  transfers between devices with their start and end apart: 4, of which 4 were waited for; matrix products, arithmetic and copies ran while one was open for 6% of the time, Pallas kernels for 0%

commit v1 on v0

v1 whole, which is shorter than its diff:
```python
import functools
import math

import jax
import jax.numpy as jnp
from jax import lax
from jax.experimental import pallas as pl
from jax.experimental.pallas import tpu as pltpu
from jax.sharding import PartitionSpec as P

HD = 128
BLK = 128
D = 4096
HB = 64
SLOTS = 8
ROWS = HB * SLOTS
SRC = 8
ALL = SRC * ROWS
HALF = HB // 2
TQ = 256
TK = 512
MESH = pl.DeviceIdType.MESH
F32 = jnp.float32
BF16 = jnp.bfloat16

OWN, L0, R0, MIR, O0, L1, R1, O1 = range(8)
CHUNKS = ((0, 0), (0, -1), (0, 1), (1, 0), (0, 2), (1, -1), (1, 1), (1, 2))
OTHERS = [(d, e) for d in range(4) for e in range(2)][1:]


def place():
    s = lax.axis_index("seq")
    t = lax.axis_index("tp")
    return s // 8, (s // 2) % 4, s % 2, t // 2, t % 2


def device(y, zl, c, x, zh):
    return ((y * 4 + zl) * 2 + c, x * 2 + zh)


def other_core(c, e):
    return 1 - c if e else c


def starts_of(block_order, y, zl, c, x, zh):
    out = []
    for mirrored, dx in CHUNKS:
        z = 3 - zl if mirrored else zl
        half = 1 - zh if mirrored else zh
        s = (y * 4 + z) * 2 + c
        row = s * ROWS + (((x + dx) % 4) * 2 + half) * HB
        out.append(row)
    rows = jnp.stack(out, axis=-1).reshape(-1)
    hit = (rows // BLK)[:, None] == jnp.arange(block_order.shape[0], dtype=jnp.int32)[None, :]
    block = jnp.sum(jnp.where(hit, block_order[None, :], 0), axis=1)
    return block * BLK + rows % BLK


def sort_chunks(starts):
    count = starts.shape[-1]
    rank = jnp.sum((starts[:, None] < starts[None, :]).astype(jnp.int32), axis=0)
    hit = rank[None, :] == jnp.arange(count, dtype=jnp.int32)[:, None]
    order = jnp.sum(jnp.where(hit, jnp.arange(count, dtype=jnp.int32)[None, :], 0), axis=1)
    first = jnp.sum(jnp.where(hit, starts[None, :], 0), axis=1)
    return order, first


def greet(peers):
    barrier = pltpu.get_barrier_semaphore()
    for peer in peers:
        pl.semaphore_signal(barrier, inc=1, device_id=peer, device_id_type=MESH)
    return barrier


def remote(src, dst, send, recv, peer):
    return pltpu.make_async_remote_copy(
        src_ref=src, dst_ref=dst, send_sem=send, recv_sem=recv, device_id=peer, device_id_type=MESH
    )


def project_kernel(
    hid, gain, w_hbm, cos, sin, q_out, kv_out,
    rows, wv, qs, kvs, w_sem, x_send, x_recv, z_send, z_recv,
    kv_send, kv_recv, q_send, q_recv, own_sem,
):
    y, zl, c, x, zh = place()
    right = device(y, zl, c, (x + 1) % 4, zh)
    left = device(y, zl, c, (x + 3) % 4, zh)
    mirror = device(y, 3 - zl, c, x, 1 - zh)
    kv_peers = [((y + d) % 4, other_core(c, e)) for d, e in OTHERS]
    q_peers = [((zl + d) % 4, other_core(c, e)) for d, e in OTHERS]
    kv_ids = [device(py, zl, pc, x, zh) for py, pc in kv_peers]
    q_ids = [device(y, pz, pc, x, zh) for pz, pc in q_peers]
    peers = [right, left, mirror] + kv_ids + q_ids[1:]
    barrier = greet(peers)
    w_copy = pltpu.make_async_copy(w_hbm, wv, w_sem)
    w_copy.start()

    floats = hid[...].astype(F32)
    scale = lax.rsqrt(jnp.mean(floats * floats, axis=-1, keepdims=True) + 1e-05)
    rows[0:HB, :] = (floats * scale * gain[...]).astype(BF16)
    pl.semaphore_wait(barrier, len(peers))

    def at(slot, lo=0, hi=HB):
        return rows.at[pl.ds(slot * HB + lo, hi - lo), :]

    def to_right(p, own, slot):
        return remote(at(own), at(slot), x_send.at[p, 0], x_recv.at[p, 0], right)

    def to_left(p, own, slot):
        return remote(at(own), at(slot), x_send.at[p, 1], x_recv.at[p, 1], left)

    def pass_right(p, src, dst):
        return remote(at(src, 0, HALF), at(dst, 0, HALF), x_send.at[p, 2], x_recv.at[p, 2], right)

    def pass_left(p, src, dst):
        return remote(at(src, HALF, HB), at(dst, HALF, HB), x_send.at[p, 3], x_recv.at[p, 3], left)

    to_mirror = remote(at(OWN), at(MIR), z_send, z_recv, mirror)
    r0, l0 = to_right(0, OWN, L0), to_left(0, OWN, R0)
    pr0, pl0 = pass_right(0, L0, O0), pass_left(0, R0, O0)
    r1, l1 = to_right(1, MIR, L1), to_left(1, MIR, R1)
    pr1, pl1 = pass_right(1, L1, O1), pass_left(1, R1, O1)

    to_mirror.start()
    r0.start()
    l0.start()
    mine = y * 2 + c
    mine_q = zl * 2 + c

    def part(ref, lo, hi, *index):
        return ref.at[(*index, pl.ds(lo, hi - lo), slice(None))]

    def work(first, last):
        lo, hi = first * HB, last * HB
        chunk = rows[lo:hi, :]
        cs, sn = cos[lo:hi, :], sin[lo:hi, :]
        q = jnp.dot(chunk, wv[0], preferred_element_type=F32)
        k = jnp.dot(chunk, wv[1], preferred_element_type=F32)
        v = jnp.dot(chunk, wv[2], preferred_element_type=F32)
        for h in range(2):
            lane = slice(h * HD, (h + 1) * HD)
            for out, cols, t in ((qs, slice(0, HD), q[:, lane]), (kvs, slice(0, HD), k[:, lane])):
                turned = t * cs + pltpu.roll(t, HD // 2, 1) * sn
                out[h, lo:hi, cols] = turned.astype(BF16)
            kvs[h, lo:hi, HD : 2 * HD] = v[:, lane].astype(BF16)
        for i, (py, pc) in enumerate(kv_peers):
            remote(
                part(kvs, lo, hi, pc), part(kv_out, lo, hi, mine),
                kv_send.at[i], kv_recv.at[mine], kv_ids[i],
            ).start()
        for i, (pz, pc) in enumerate(q_peers):
            remote(
                part(qs, lo, hi, pc), part(q_out, lo, hi, mine_q),
                q_send.at[i], q_recv.at[mine_q], q_ids[i],
            ).start()

    w_copy.wait()
    work(OWN, OWN + 1)
    r0.wait_recv()
    pr0.start()
    l0.wait_recv()
    pl0.start()
    work(L0, R0 + 1)
    to_mirror.wait_recv()
    r1.start()
    l1.start()
    pr0.wait_recv()
    pl0.wait_recv()
    work(MIR, O0 + 1)
    r1.wait_recv()
    pr1.start()
    l1.wait_recv()
    pl1.start()
    work(L1, R1 + 1)
    pr1.wait_recv()
    pl1.wait_recv()
    work(O1, O1 + 1)
    own_kv = pltpu.make_async_copy(kvs.at[c], kv_out.at[mine], own_sem.at[0])
    own_q = pltpu.make_async_copy(qs.at[c], q_out.at[mine_q], own_sem.at[1])
    own_kv.start()
    own_q.start()
    for copy in (to_mirror, r0, l0, pr0, pl0, r1, l1, pr1, pl1):
        copy.wait_send()
    for i, (py, pc) in enumerate(kv_peers):
        src = py * 2 + pc
        done = remote(kvs.at[pc], kv_out.at[src], kv_send.at[i], kv_recv.at[src], kv_ids[i])
        done.wait_send()
        done.wait_recv()
    for i, (pz, pc) in enumerate(q_peers):
        src = pz * 2 + pc
        done = remote(qs.at[pc], q_out.at[src], q_send.at[i], q_recv.at[src], q_ids[i])
        done.wait_send()
        done.wait_recv()
    own_kv.wait()
    own_q.wait()


def project(hidden_in, norm_gain, weight, cos, sin):
    vmem = pl.BlockSpec(memory_space=pltpu.VMEM)
    hbm = pl.BlockSpec(memory_space=pl.ANY)
    dma = pltpu.SemaphoreType.DMA
    return pl.pallas_call(
        project_kernel,
        out_shape=(
            jax.ShapeDtypeStruct((SRC, ROWS, HD), BF16),
            jax.ShapeDtypeStruct((SRC, ROWS, 2 * HD), BF16),
        ),
        in_specs=[vmem, vmem, hbm, vmem, vmem],
        out_specs=(hbm, hbm),
        scratch_shapes=[
            pltpu.VMEM((ROWS, D), BF16),
            pltpu.VMEM((3, D, 2 * HD), BF16),
            pltpu.VMEM((2, ROWS, HD), BF16),
            pltpu.VMEM((2, ROWS, 2 * HD), BF16),
            dma, dma((2, 4)), dma((2, 4)), dma, dma,
            dma((SRC,)), dma((SRC,)), dma((SRC,)), dma((SRC,)), dma((2,)),
        ],
        compiler_params=pltpu.CompilerParams(
            collective_id=0, has_side_effects=True, vmem_limit_bytes=40 << 20
        ),
        name="project",
    )(hidden_in, norm_gain, weight, cos, sin)


def attend_kernel(meta, q_hbm, kv_hbm, o_out, lse_out, qs, ks, va, scores, top, sems):
    chunks = ALL // HB

    @pl.loop(0, chunks)
    def _(r):
        rows = pl.ds(pl.multiple_of(r * HB, HB), HB)
        oq, ok = meta[0, r], meta[1, r]
        pltpu.make_async_copy(q_hbm.at[oq], qs.at[rows, :], sems.at[0]).start()
        pltpu.make_async_copy(kv_hbm.at[ok, :, 0:HD], ks.at[rows, :], sems.at[1]).start()
        pltpu.make_async_copy(
            kv_hbm.at[ok, :, HD : 2 * HD], va.at[rows, 0:HD], sems.at[2]
        ).start()

    va[:, HD : 2 * HD] = jnp.ones((ALL, HD), BF16)
    pltpu.make_async_copy(qs, qs, sems.at[0]).wait()
    pltpu.make_async_copy(ks, ks, sems.at[1]).wait()
    pltpu.make_async_copy(ks, va.at[:, 0:HD], sems.at[2]).wait()
    scale = math.log2(math.e) / HD**0.5
    per_q, per_k = TQ // HB, TK // HB

    @pl.loop(0, ALL // TQ)
    def _(i):
        q = qs[pl.ds(pl.multiple_of(i * TQ, TQ), TQ), :]
        qmin = meta[2, i * per_q]
        qmax = meta[2, i * per_q + per_q - 1] + HB - 1
        n_all = jnp.int32(0)
        n_full = jnp.int32(0)
        for j in range(ALL // TK):
            n_all += (meta[3, j * per_k] <= qmax).astype(jnp.int32)
            n_full += (meta[3, j * per_k + per_k - 1] + HB - 1 <= qmin).astype(jnp.int32)
        top[...] = jnp.full((TQ, HD), -1e29, F32)

        def score(j, masked):
            at = pl.ds(pl.multiple_of(j * TK, TK), TK)
            s = lax.dot_general(
                q, ks[at, :], (((1,), (1,)), ((), ())), preferred_element_type=F32
            )
            if masked:
                row = lax.broadcasted_iota(jnp.int32, (TQ, 1), 0)
                col = lax.broadcasted_iota(jnp.int32, (1, TK), 1)
                qpos, kpos = row, col
                for u in range(per_q):
                    qpos = jnp.where(row // HB == u, meta[2, i * per_q + u] + row % HB, qpos)
                for u in range(per_k):
                    kpos = jnp.where(col // HB == u, meta[3, j * per_k + u] + col % HB, kpos)
                s = jnp.where(kpos <= qpos, s, -1e30)
            scores[:, at] = s
            best = top[...]
            for u in range(TK // HD):
                best = jnp.maximum(best, s[:, u * HD : (u + 1) * HD])
            top[...] = best

        pl.loop(0, n_full)(lambda j: score(j, False))
        pl.loop(n_full, n_all)(lambda j: score(j, True))
        best = jnp.max(top[...], axis=1, keepdims=True)

        def step(j, acc):
            at = pl.ds(pl.multiple_of(j * TK, TK), TK)
            weight = jnp.exp2((scores[:, at] - best) * scale).astype(BF16)
            return acc + jnp.dot(weight, va[at, :], preferred_element_type=F32)

        acc = lax.fori_loop(0, n_all, step, jnp.zeros((TQ, 2 * HD), F32))
        total = acc[:, HD:]
        some = total > 0
        out = jnp.where(some, acc[:, :HD] / jnp.where(some, total, 1.0), 0.0).astype(BF16)
        lse = jnp.where(some, best * scale + jnp.log2(jnp.where(some, total, 1.0)), -1e30)
        lanes = lse.T
        for u in range(per_q):
            oq = meta[0, i * per_q + u]
            o_out[oq] = out[u * HB : (u + 1) * HB, :]
            lse_out[oq // SLOTS, pl.ds(oq % SLOTS, 1), 0:HB] = lanes[0:1, u * HB : (u + 1) * HB]


def attend(meta, q, kv):
    vmem = pl.BlockSpec(memory_space=pltpu.VMEM)
    hbm = pl.BlockSpec(memory_space=pl.ANY)
    chunks = ALL // HB
    return pl.pallas_call(
        attend_kernel,
        out_shape=(
            jax.ShapeDtypeStruct((chunks, HB, HD), BF16),
            jax.ShapeDtypeStruct((SRC, SLOTS, HD), F32),
        ),
        in_specs=[pl.BlockSpec(memory_space=pltpu.SMEM), hbm, hbm],
        out_specs=(vmem, vmem),
        scratch_shapes=[
            pltpu.VMEM((ALL, HD), BF16),
            pltpu.VMEM((ALL, HD), BF16),
            pltpu.VMEM((ALL, 2 * HD), BF16),
            pltpu.VMEM((TQ, ALL), F32),
            pltpu.VMEM((TQ, HD), F32),
            pltpu.SemaphoreType.DMA((3,)),
        ],
        compiler_params=pltpu.CompilerParams(vmem_limit_bytes=40 << 20),
        name="attend",
    )(meta, q.reshape(chunks, HB, HD), kv.reshape(chunks, HB, 2 * HD))


def combine_kernel(
    o_hbm, lse_in, w_ref, out_ref,
    parts, lses, ctx, terms, halves, fulls, mirrored,
    o_send, o_recv, l_send, l_recv, own_sem, h_send, h_recv, f_send, f_recv, z_send, z_recv,
):
    y, zl, c, x, zh = place()
    right = device(y, zl, c, (x + 1) % 4, zh)
    left = device(y, zl, c, (x + 3) % 4, zh)
    mirror = device(y, 3 - zl, c, x, 1 - zh)
    peers = [((zl + d) % 4, other_core(c, e)) for d, e in OTHERS]
    ids = [device(y, pz, pc, x, zh) for pz, pc in peers]
    mine = zl * 2 + c
    barrier = greet([right, left, mirror] + ids)
    own_o = pltpu.make_async_copy(o_hbm.at[mine], parts.at[mine], own_sem.at[0])
    own_l = pltpu.make_async_copy(lse_in.at[mine], lses.at[mine], own_sem.at[1])
    own_o.start()
    own_l.start()
    pl.semaphore_wait(barrier, len(ids) + 3)
    for i, (pz, pc) in enumerate(peers):
        to = pz * 2 + pc
        remote(lse_in.at[to], lses.at[mine], l_send.at[i], l_recv.at[mine], ids[i]).start()
        remote(o_hbm.at[to], parts.at[mine], o_send.at[i], o_recv.at[mine], ids[i]).start()
    own_o.wait()
    own_l.wait()
    for i, (pz, pc) in enumerate(peers):
        src = pz * 2 + pc
        for done in (
            remote(lse_in.at[src], lses.at[src], l_send.at[i], l_recv.at[src], ids[i]),
            remote(o_hbm.at[src], parts.at[src], o_send.at[i], o_recv.at[src], ids[i]),
        ):
            done.wait_send()
            done.wait_recv()

    stats = lses[...].reshape(SRC * SLOTS, HD)
    stats = jnp.concatenate([stats, stats], axis=0).T
    for slot in range(SLOTS):
        lo, hi = slot * HB, (slot + 1) * HB
        for h in range(2):
            cols = [stats[0:HB, (z * 2 + h) * SLOTS + slot : (z * 2 + h) * SLOTS + slot + 1] for z in range(4)]
            best = jnp.maximum(jnp.maximum(cols[0], cols[1]), jnp.maximum(cols[2], cols[3]))
            shares = [jnp.exp2(col - best) for col in cols]
            total = shares[0] + shares[1] + shares[2] + shares[3]
            mixed = jnp.zeros((HB, HD), F32)
            for z in range(4):
                mixed += (shares[z] / total) * parts[z * 2 + h, lo:hi, :].astype(F32)
            ctx[lo:hi, h * HD : (h + 1) * HD] = mixed.astype(BF16)

    def term(slot):
        lo, hi = slot * HB, (slot + 1) * HB
        terms[lo:hi, :] = jnp.dot(ctx[lo:hi, :], w_ref[...], preferred_element_type=F32).astype(BF16)

    def at(slot, lo=0, hi=HB):
        return terms.at[pl.ds(slot * HB + lo, hi - lo), :]

    def half_right(p, slot):
        return remote(at(slot, 0, HALF), halves.at[p, 0], h_send.at[p, 0], h_recv.at[p, 0], right)

    def half_left(p, slot):
        return remote(at(slot, HALF, HB), halves.at[p, 1], h_send.at[p, 1], h_recv.at[p, 1], left)

    def full_right(p, slot):
        return remote(at(slot), fulls.at[p, 0], f_send.at[p, 0], f_recv.at[p, 0], right)

    def full_left(p, slot):
        return remote(at(slot), fulls.at[p, 1], f_send.at[p, 1], f_recv.at[p, 1], left)

    def add(lo, hi, more):
        terms[lo:hi, :] = (terms[lo:hi, :].astype(F32) + more.astype(F32)).astype(BF16)

    slots = ((L0, R0, O0), (L1, R1, O1))
    started = []
    chains = {}
    for p in (1, 0):
        left_slot, right_slot, far = slots[p]
        term(far)
        hr, hl = half_right(p, far), half_left(p, far)
        hr.start()
        hl.start()
        chains[p] = (hr, hl)
        started += [hr, hl]
    for p in (1, 0):
        left_slot, right_slot, far = slots[p]
        hr, hl = chains[p]
        term(left_slot)
        term(right_slot)
        hr.wait_recv()
        add(right_slot * HB, right_slot * HB + HALF, halves[p, 0])
        fr = full_right(p, right_slot)
        fr.start()
        hl.wait_recv()
        add(left_slot * HB + HALF, left_slot * HB + HB, halves[p, 1])
        fl = full_left(p, left_slot)
        fl.start()
        chains[p] = (fr, fl)
        started += [fr, fl]
    term(MIR)
    term(OWN)
    for copy in chains[1]:
        copy.wait_recv()
    add(MIR * HB, MIR * HB + HB, fulls[1, 0].astype(F32) + fulls[1, 1].astype(F32))
    to_mirror = remote(at(MIR), mirrored, z_send, z_recv, mirror)
    to_mirror.start()
    for copy in chains[0]:
        copy.wait_recv()
    to_mirror.wait_recv()
    total = terms[0:HB, :].astype(F32) + fulls[0, 0].astype(F32)
    total = total + fulls[0, 1].astype(F32) + mirrored[...].astype(F32)
    out_ref[...] = total.astype(BF16)
    for copy in started:
        copy.wait_send()
    to_mirror.wait_send()


def combine(o, lse, out_weight):
    vmem = pl.BlockSpec(memory_space=pltpu.VMEM)
    hbm = pl.BlockSpec(memory_space=pl.ANY)
    dma = pltpu.SemaphoreType.DMA
    return pl.pallas_call(
        combine_kernel,
        out_shape=jax.ShapeDtypeStruct((HB, D), BF16),
        in_specs=[hbm, hbm, vmem],
        out_specs=vmem,
        scratch_shapes=[
            pltpu.VMEM((SRC, ROWS, HD), BF16),
            pltpu.VMEM((SRC, SLOTS, HD), F32),
            pltpu.VMEM((ROWS, 2 * HD), BF16),
            pltpu.VMEM((ROWS, D), BF16),
            pltpu.VMEM((2, 2, HALF, D), BF16),
            pltpu.VMEM((2, 2, HB, D), BF16),
            pltpu.VMEM((HB, D), BF16),
            dma((SRC,)), dma((SRC,)), dma((SRC,)), dma((SRC,)), dma((2,)),
            dma((2, 2)), dma((2, 2)), dma((2, 2)), dma((2, 2)), dma, dma,
        ],
        compiler_params=pltpu.CompilerParams(
            collective_id=1, has_side_effects=True, vmem_limit_bytes=40 << 20
        ),
        name="combine",
    )(o.reshape(SRC, ROWS, HD), lse, out_weight)


def local(hidden_in, norm_gain, qkv_weight, out_weight, block_order):
    y, zl, c, x, zh = place()
    zero = jnp.zeros((4, 2), jnp.int32)
    lane = jnp.arange(4, dtype=jnp.int32)[:, None] + zero
    core = jnp.arange(2, dtype=jnp.int32)[None, :] + zero
    q_starts = starts_of(block_order, zero + y, lane, core, x, zh)
    k_starts = starts_of(block_order, lane, zero + zl, core, x, zh)
    q_order, q_first = sort_chunks(q_starts)
    k_order, k_first = sort_chunks(k_starts)
    meta = jnp.stack([q_order, k_order, q_first, k_first])

    mine = starts_of(block_order, y, zl, c, x, zh)
    position = (mine[:, None] + jnp.arange(HB, dtype=jnp.int32)[None, :]).reshape(-1)
    inv_freq = 10000.0 ** (-(jnp.arange(HD // 2, dtype=F32) * 2.0 / HD))
    angle = position.astype(F32)[:, None] * inv_freq[None, :]
    cosine, sine = jnp.cos(angle), jnp.sin(angle)
    cos = jnp.concatenate([cosine, cosine], axis=1)
    sin = jnp.concatenate([-sine, sine], axis=1)

    weight = jnp.transpose(qkv_weight, (1, 0, 2))
    q, kv = project(hidden_in, norm_gain[None, :], weight, cos, sin)
    o, lse = attend(meta, q, kv)
    return combine(o, lse, out_weight)


def solution(mesh):
    in_specs = (P(("seq", "tp"), None), P(), P(None, None, "tp"), P("tp", None), P())
    out_specs = P(("seq", "tp"), None)
    return jax.shard_map(local, mesh=mesh, in_specs=in_specs, out_specs=out_specs, check_vma=False)
```

time: 631 us -> 194 us (0.31)
  the two profiles are of different devices: /device:TPU:33 before, /device:TPU:1 now
where the time goes in v1:
time: 194 us
  Pallas kernels  186 us (96%)
  local copies, waits for them, and re-layouts  4.11 us (2%)
  other arithmetic  3.71 us (2%)
    pallas_call x1, Pallas kernels, combine(): pl.pallas_call(combine_kernel, out_shape=jax.ShapeDtypeStruct((HB, D), BF...  78.5 us
    pallas_call x1, Pallas kernels, project(): pl.pallas_call(project_kernel, out_shape=(jax.ShapeDtypeStruct((SRC, ROWS...  61.9 us
    pallas_call x1, Pallas kernels, attend(): pl.pallas_call(attend_kernel, out_shape=(jax.ShapeDtypeStruct((chunks, HB...  45.2 us

profile of v1, /device:TPU:1, one launch (start us, length us, event | category | flops | bytes accessed | tf_op | source)
XLA Modules:
  0.0 193.6 jit_solution(10746417913976638940)
XLA Ops:
  0.0 0.0 copy-start.3
  0.0 0.0 copy-start.2
  0.0 0.1 stack.79
  0.1 0.9 select_reduce_fusion.6
  1.0 0.1 add_convert_fusion
  1.1 0.1 convert_element_type.19
  1.4 0.1 copy.6
  1.5 0.1 reshape.1045
  1.6 0.1 copy.7
  1.7 0.1 reshape.1046
  1.8 0.8 select_reduce_fusion.5
  2.7 0.1 convert_reduce_fusion
  2.8 0.1 select_reduce_fusion.2
  2.9 0.1 convert_reduce_fusion.1
  3.0 0.1 select_reduce_fusion.4
  3.1 1.0 fusion
  4.1 0.2 pad_maximum_fusion
  4.3 0.0 copy-done.3
  4.3 0.0 copy-done.2
  4.4 0.0 copy-start
  4.4 2.8 %copy-done = bf16[4096,3,256]{2,0,1:T(8,128)(2,1)S(1)} copy-done((bf16[4096,3,256]{2,0,1:T(8,128)(2,1)S(1)}, bf16[4096,3,256]{2,0,1:T(8,128)(2,1)}, u32[]{:S(2)}) %copy-start) | copy-done | bytes 6291480
  7.1 61.9 %project.1 = (bf16[8,512,128]{2,1,0:T(8,128)(2,1)S(1)}, bf16[8,512,256]{2,1,0:T(8,128)(2,1)S(1)}) custom-call(bf16[64,4096]{1,0:T(8,128)(2,1)S(1)} %copy-done.2, f32[1,4096]{1,0:T(1,128)S(1)} %bitcast.21, bf16[3,4096,256]{2,1,0:T(8,128)(2,1)S(1)} %bitcast.17, f32[512,128]{1,0:T(8,128)S(1)} %get-tuple-element.24.cos, f32[512,128]{1,0:T(8,128)S(1)} %get-tuple-element.25.sin), custom_call_target="tpu_custom_call" | custom-call | tf_op jit(solution)/shard_map/project/pallas_call | solution.py:203
  69.0 0.0 copy-start.1
  69.0 45.2 %attend.1 = (bf16[64,64,128]{2,1,0:T(8,128)(2,1)S(1)}, f32[8,8,128]{2,1,0:T(8,128)S(1)}) custom-call(s32[4,64]{1,0:T(4,128)S(1)} %pad_add_fusion.meta, bf16[64,64,128]{2,1,0:T(8,128)(2,1)S(1)} %bitcast.20, bf16[64,64,256]{2,1,0:T(8,128)(2,1)S(1)} %bitcast.18), custom_call_target="tpu_custom_call" | custom-call | tf_op jit(solution)/shard_map/attend/pallas_call | solution.py:303
  114.2 0.0 copy-done.1
  114.3 78.5 %combine.1 = bf16[64,4096]{1,0:T(8,128)(2,1)S(1)} custom-call(bf16[8,512,128]{2,1,0:T(8,128)(2,1)S(1)} %bitcast.19, f32[8,8,128]{2,1,0:T(8,128)S(1)} %get-tuple-element.12.lse_in, bf16[256,4096]{1,0:T(8,128)(2,1)S(1)} %copy-done.1), custom_call_target="tpu_custom_call" | custom-call | tf_op jit(solution)/shard_map/combine/pallas_call | solution.py:441
  192.8 0.8 copy.23
  (27 shorter events, 0.3 us)
Async XLA Ops:
  0.0 4.3 %copy-start.3 = (f32[4096]{0:T(1024)S(1)}, f32[4096]{0:T(1024)}, u32[]{:S(2)}) copy-start(f32[4096]{0:T(1024)} %param.6) | copy-start | bytes 49156
  0.0 4.3 %copy-start.2 = (bf16[64,4096]{1,0:T(8,128)(2,1)S(1)}, bf16[64,4096]{1,0:T(8,128)(2,1)}, u32[]{:S(2)}) copy-start(bf16[64,4096]{1,0:T(8,128)(2,1)} %hid.1) | copy-start | bytes 1572868
  4.4 2.8 %copy-start = (bf16[4096,3,256]{2,0,1:T(8,128)(2,1)S(1)}, bf16[4096,3,256]{2,0,1:T(8,128)(2,1)}, u32[]{:S(2)}) copy-start(bf16[4096,3,256]{2,0,1:T(8,128)(2,1)} %param.7) | copy-start | bytes 18874372
  69.0 45.2 %copy-start.1 = (bf16[256,4096]{1,0:T(8,128)(2,1)S(1)}, bf16[256,4096]{1,0:T(8,128)(2,1)}, u32[]{:S(2)}) copy-start(bf16[256,4096]{1,0:T(8,128)(2,1)} %w_ref.1) | copy-start | bytes 6291460

commit v2 on v1

--- a/solution.py
+++ b/solution.py
@@ -1,8 +1,8 @@
-import functools
 import math
 
 import jax
 import jax.numpy as jnp
+import numpy as np
 from jax import lax
 from jax.experimental import pallas as pl
 from jax.experimental.pallas import tpu as pltpu
@@ -17,14 +17,16 @@
 SRC = 8
 ALL = SRC * ROWS
 HALF = HB // 2
-TQ = 256
-TK = 512
+TQ = 512
+TK = 1024
 MESH = pl.DeviceIdType.MESH
 F32 = jnp.float32
 BF16 = jnp.bfloat16
 
 OWN, L0, R0, MIR, O0, L1, R1, O1 = range(8)
 CHUNKS = ((0, 0), (0, -1), (0, 1), (1, 0), (0, 2), (1, -1), (1, 1), (1, 2))
+SCALE = math.log2(math.e) / HD**0.5
+GROUPS = ((O1, O1 + 1), (L1, R1 + 1), (MIR, MIR + 1), (O0, O0 + 1), (L0, R0 + 1), (OWN, OWN + 1))
 OTHERS = [(d, e) for d in range(4) for e in range(2)][1:]
 
 
@@ -43,25 +45,28 @@
 
 
 def starts_of(block_order, y, zl, c, x, zh):
-    out = []
-    for mirrored, dx in CHUNKS:
-        z = 3 - zl if mirrored else zl
-        half = 1 - zh if mirrored else zh
-        s = (y * 4 + z) * 2 + c
-        row = s * ROWS + (((x + dx) % 4) * 2 + half) * HB
-        out.append(row)
-    rows = jnp.stack(out, axis=-1).reshape(-1)
-    hit = (rows // BLK)[:, None] == jnp.arange(block_order.shape[0], dtype=jnp.int32)[None, :]
-    block = jnp.sum(jnp.where(hit, block_order[None, :], 0), axis=1)
-    return block * BLK + rows % BLK
+    index = np.arange(2 * SRC * SLOTS + SLOTS)
+    of_q, of_k = index < SRC * SLOTS, (index >= SRC * SLOTS) & (index < 2 * SRC * SLOTS)
+    lane, core, slot = index // (2 * SLOTS) % 4, index // SLOTS % 2, index % SLOTS
+    mirrored = np.array([m for m, _ in CHUNKS])[slot]
+    shift = np.array([dx for _, dx in CHUNKS])[slot] % 4
+    py = jnp.where(of_k, lane, y)
+    pz = jnp.where(of_q, lane, zl)
+    pc = jnp.where(of_q | of_k, core, c)
+    pz = jnp.where(mirrored == 1, 3 - pz, pz)
+    half = jnp.where(mirrored == 1, 1 - zh, zh)
+    block = ((py * 4 + pz) * 2 + pc) * (ROWS // BLK) + ((x + shift) & 3)
+    hit = block[:, None] == jnp.arange(block_order.shape[0], dtype=jnp.int32)[None, :]
+    return jnp.sum(jnp.where(hit, block_order[None, :], 0), axis=1) * BLK + half * HB
 
 
 def sort_chunks(starts):
     count = starts.shape[-1]
-    rank = jnp.sum((starts[:, None] < starts[None, :]).astype(jnp.int32), axis=0)
-    hit = rank[None, :] == jnp.arange(count, dtype=jnp.int32)[:, None]
-    order = jnp.sum(jnp.where(hit, jnp.arange(count, dtype=jnp.int32)[None, :], 0), axis=1)
-    first = jnp.sum(jnp.where(hit, starts[None, :], 0), axis=1)
+    index = jnp.arange(count, dtype=jnp.int32)
+    rank = jnp.sum((starts[:, :, None] < starts[:, None, :]).astype(jnp.int32), axis=1)
+    hit = rank[:, None, :] == index[None, :, None]
+    order = jnp.sum(jnp.where(hit, index[None, None, :], 0), axis=2)
+    first = jnp.sum(jnp.where(hit, starts[:, None, :], 0), axis=2)
     return order, first
 
 
@@ -104,27 +109,28 @@
     def at(slot, lo=0, hi=HB):
         return rows.at[pl.ds(slot * HB + lo, hi - lo), :]
 
-    def to_right(p, own, slot):
-        return remote(at(own), at(slot), x_send.at[p, 0], x_recv.at[p, 0], right)
-
-    def to_left(p, own, slot):
-        return remote(at(own), at(slot), x_send.at[p, 1], x_recv.at[p, 1], left)
-
-    def pass_right(p, src, dst):
-        return remote(at(src, 0, HALF), at(dst, 0, HALF), x_send.at[p, 2], x_recv.at[p, 2], right)
-
-    def pass_left(p, src, dst):
-        return remote(at(src, HALF, HB), at(dst, HALF, HB), x_send.at[p, 3], x_recv.at[p, 3], left)
-
-    to_mirror = remote(at(OWN), at(MIR), z_send, z_recv, mirror)
-    r0, l0 = to_right(0, OWN, L0), to_left(0, OWN, R0)
-    pr0, pl0 = pass_right(0, L0, O0), pass_left(0, R0, O0)
-    r1, l1 = to_right(1, MIR, L1), to_left(1, MIR, R1)
-    pr1, pl1 = pass_right(1, L1, O1), pass_left(1, R1, O1)
-
-    to_mirror.start()
-    r0.start()
-    l0.start()
+    def step(p, kind, src, dst, lo, hi, peer):
+        return remote(at(src, lo, hi), at(dst, lo, hi), x_send.at[p, kind], x_recv.at[p, kind], peer)
+
+    def ring(p, src, from_left, from_right, far):
+        return (
+            step(p, 0, src, from_left, 0, HALF, right),
+            step(p, 1, src, from_right, HALF, HB, left),
+            step(p, 2, src, from_left, HALF, HB, right),
+            step(p, 3, src, from_right, 0, HALF, left),
+            step(p, 4, from_left, far, 0, HALF, right),
+            step(p, 5, from_right, far, HALF, HB, left),
+        )
+
+    mirror_lo = remote(at(OWN, 0, HALF), at(MIR, 0, HALF), z_send.at[0], z_recv.at[0], mirror)
+    mirror_hi = remote(at(OWN, HALF, HB), at(MIR, HALF, HB), z_send.at[1], z_recv.at[1], mirror)
+    near = ring(0, OWN, L0, R0, O0)
+    far = ring(1, MIR, L1, R1, O1)
+
+    mirror_lo.start()
+    mirror_hi.start()
+    for copy in near[:4]:
+        copy.start()
     mine = y * 2 + c
     mine_q = zl * 2 + c
 
@@ -140,9 +146,9 @@
         v = jnp.dot(chunk, wv[2], preferred_element_type=F32)
         for h in range(2):
             lane = slice(h * HD, (h + 1) * HD)
-            for out, cols, t in ((qs, slice(0, HD), q[:, lane]), (kvs, slice(0, HD), k[:, lane])):
+            for out, by, t in ((qs, SCALE, q[:, lane]), (kvs, 1.0, k[:, lane])):
                 turned = t * cs + pltpu.roll(t, HD // 2, 1) * sn
-                out[h, lo:hi, cols] = turned.astype(BF16)
+                out[h, lo:hi, 0:HD] = (turned * by).astype(BF16)
             kvs[h, lo:hi, HD : 2 * HD] = v[:, lane].astype(BF16)
         for i, (py, pc) in enumerate(kv_peers):
             remote(
@@ -157,30 +163,38 @@
 
     w_copy.wait()
     work(OWN, OWN + 1)
-    r0.wait_recv()
-    pr0.start()
-    l0.wait_recv()
-    pl0.start()
+    near[0].wait_recv()
+    near[4].start()
+    near[1].wait_recv()
+    near[5].start()
+    near[2].wait_recv()
+    near[3].wait_recv()
     work(L0, R0 + 1)
-    to_mirror.wait_recv()
-    r1.start()
-    l1.start()
-    pr0.wait_recv()
-    pl0.wait_recv()
-    work(MIR, O0 + 1)
-    r1.wait_recv()
-    pr1.start()
-    l1.wait_recv()
-    pl1.start()
+    mirror_lo.wait_recv()
+    far[0].start()
+    far[3].start()
+    near[4].wait_recv()
+    near[5].wait_recv()
+    work(O0, O0 + 1)
+    mirror_hi.wait_recv()
+    far[1].start()
+    far[2].start()
+    work(MIR, MIR + 1)
+    far[0].wait_recv()
+    far[4].start()
+    far[1].wait_recv()
+    far[5].start()
+    far[2].wait_recv()
+    far[3].wait_recv()
     work(L1, R1 + 1)
-    pr1.wait_recv()
-    pl1.wait_recv()
+    far[4].wait_recv()
+    far[5].wait_recv()
     work(O1, O1 + 1)
     own_kv = pltpu.make_async_copy(kvs.at[c], kv_out.at[mine], own_sem.at[0])
     own_q = pltpu.make_async_copy(qs.at[c], q_out.at[mine_q], own_sem.at[1])
     own_kv.start()
     own_q.start()
-    for copy in (to_mirror, r0, l0, pr0, pl0, r1, l1, pr1, pl1):
+    for copy in (mirror_lo, mirror_hi, *near, *far):
         copy.wait_send()
     for i, (py, pc) in enumerate(kv_peers):
         src = py * 2 + pc
@@ -213,11 +227,11 @@
             pltpu.VMEM((3, D, 2 * HD), BF16),
             pltpu.VMEM((2, ROWS, HD), BF16),
             pltpu.VMEM((2, ROWS, 2 * HD), BF16),
-            dma, dma((2, 4)), dma((2, 4)), dma, dma,
+            dma, dma((2, 6)), dma((2, 6)), dma((2,)), dma((2,)),
             dma((SRC,)), dma((SRC,)), dma((SRC,)), dma((SRC,)), dma((2,)),
         ],
         compiler_params=pltpu.CompilerParams(
-            collective_id=0, has_side_effects=True, vmem_limit_bytes=40 << 20
+            collective_id=0, has_side_effects=True, vmem_limit_bytes=60 << 20
         ),
         name="project",
     )(hidden_in, norm_gain, weight, cos, sin)
@@ -240,7 +254,6 @@
     pltpu.make_async_copy(qs, qs, sems.at[0]).wait()
     pltpu.make_async_copy(ks, ks, sems.at[1]).wait()
     pltpu.make_async_copy(ks, va.at[:, 0:HD], sems.at[2]).wait()
-    scale = math.log2(math.e) / HD**0.5
     per_q, per_k = TQ // HB, TK // HB
 
     @pl.loop(0, ALL // TQ)
@@ -281,14 +294,14 @@
 
         def step(j, acc):
             at = pl.ds(pl.multiple_of(j * TK, TK), TK)
-            weight = jnp.exp2((scores[:, at] - best) * scale).astype(BF16)
+            weight = jnp.exp2(scores[:, at] - best).astype(BF16)
             return acc + jnp.dot(weight, va[at, :], preferred_element_type=F32)
 
         acc = lax.fori_loop(0, n_all, step, jnp.zeros((TQ, 2 * HD), F32))
         total = acc[:, HD:]
         some = total > 0
         out = jnp.where(some, acc[:, :HD] / jnp.where(some, total, 1.0), 0.0).astype(BF16)
-        lse = jnp.where(some, best * scale + jnp.log2(jnp.where(some, total, 1.0)), -1e30)
+        lse = jnp.where(some, best + jnp.log2(jnp.where(some, total, 1.0)), -1e30)
         lanes = lse.T
         for u in range(per_q):
             oq = meta[0, i * per_q + u]
@@ -316,15 +329,15 @@
             pltpu.VMEM((TQ, HD), F32),
             pltpu.SemaphoreType.DMA((3,)),
         ],
-        compiler_params=pltpu.CompilerParams(vmem_limit_bytes=40 << 20),
+        compiler_params=pltpu.CompilerParams(vmem_limit_bytes=60 << 20),
         name="attend",
     )(meta, q.reshape(chunks, HB, HD), kv.reshape(chunks, HB, 2 * HD))
 
 
 def combine_kernel(
-    o_hbm, lse_in, w_ref, out_ref,
-    parts, lses, ctx, terms, halves, fulls, mirrored,
-    o_send, o_recv, l_send, l_recv, own_sem, h_send, h_recv, f_send, f_recv, z_send, z_recv,
+    o_hbm, lse_in, w_hbm, out_ref,
+    w_ref, parts, lses, ctx, terms, halves, fulls, mirrored,
+    w_sem, o_send, o_recv, l_send, l_recv, own_sem, h_send, h_recv, f_send, f_recv, z_send, z_recv,
 ):
     y, zl, c, x, zh = place()
     right = device(y, zl, c, (x + 1) % 4, zh)
@@ -338,100 +351,130 @@
     own_l = pltpu.make_async_copy(lse_in.at[mine], lses.at[mine], own_sem.at[1])
     own_o.start()
     own_l.start()
+    w_copy = pltpu.make_async_copy(w_hbm, w_ref, w_sem)
+    w_copy.start()
     pl.semaphore_wait(barrier, len(ids) + 3)
     for i, (pz, pc) in enumerate(peers):
         to = pz * 2 + pc
         remote(lse_in.at[to], lses.at[mine], l_send.at[i], l_recv.at[mine], ids[i]).start()
-        remote(o_hbm.at[to], parts.at[mine], o_send.at[i], o_recv.at[mine], ids[i]).start()
+
+    def o_rows(ref, index, group):
+        first, last = GROUPS[group]
+        return ref.at[index, pl.ds(first * HB, (last - first) * HB), :]
+
+    for group in range(len(GROUPS)):
+        for i, (pz, pc) in enumerate(peers):
+            remote(
+                o_rows(o_hbm, pz * 2 + pc, group), o_rows(parts, mine, group),
+                o_send.at[i], o_recv.at[group, mine], ids[i],
+            ).start()
     own_o.wait()
     own_l.wait()
+    w_copy.wait()
     for i, (pz, pc) in enumerate(peers):
         src = pz * 2 + pc
-        for done in (
-            remote(lse_in.at[src], lses.at[src], l_send.at[i], l_recv.at[src], ids[i]),
-            remote(o_hbm.at[src], parts.at[src], o_send.at[i], o_recv.at[src], ids[i]),
-        ):
-            done.wait_send()
-            done.wait_recv()
+        remote(lse_in.at[src], lses.at[src], l_send.at[i], l_recv.at[src], ids[i]).wait()
 
     stats = lses[...].reshape(SRC * SLOTS, HD)
     stats = jnp.concatenate([stats, stats], axis=0).T
-    for slot in range(SLOTS):
-        lo, hi = slot * HB, (slot + 1) * HB
-        for h in range(2):
-            cols = [stats[0:HB, (z * 2 + h) * SLOTS + slot : (z * 2 + h) * SLOTS + slot + 1] for z in range(4)]
-            best = jnp.maximum(jnp.maximum(cols[0], cols[1]), jnp.maximum(cols[2], cols[3]))
-            shares = [jnp.exp2(col - best) for col in cols]
-            total = shares[0] + shares[1] + shares[2] + shares[3]
-            mixed = jnp.zeros((HB, HD), F32)
-            for z in range(4):
-                mixed += (shares[z] / total) * parts[z * 2 + h, lo:hi, :].astype(F32)
-            ctx[lo:hi, h * HD : (h + 1) * HD] = mixed.astype(BF16)
-
-    def term(slot):
-        lo, hi = slot * HB, (slot + 1) * HB
+
+    def term(group):
+        for i, (pz, pc) in enumerate(peers):
+            src = pz * 2 + pc
+            remote(
+                o_rows(o_hbm, src, group), o_rows(parts, src, group),
+                o_send.at[i], o_recv.at[group, src], ids[i],
+            ).wait_recv()
+        first, last = GROUPS[group]
+        for slot in range(first, last):
+            lo, hi = slot * HB, (slot + 1) * HB
+            for h in range(2):
+                at = [(z * 2 + h) * SLOTS + slot for z in range(4)]
+                cols = [stats[0:HB, i : i + 1] for i in at]
+                best = jnp.maximum(jnp.maximum(cols[0], cols[1]), jnp.maximum(cols[2], cols[3]))
+                shares = [jnp.exp2(col - best) for col in cols]
+                total = shares[0] + shares[1] + shares[2] + shares[3]
+                mixed = jnp.zeros((HB, HD), F32)
+                for z in range(4):
+                    mixed += (shares[z] / total) * parts[z * 2 + h, lo:hi, :].astype(F32)
+                ctx[lo:hi, h * HD : (h + 1) * HD] = mixed.astype(BF16)
+        lo, hi = first * HB, last * HB
         terms[lo:hi, :] = jnp.dot(ctx[lo:hi, :], w_ref[...], preferred_element_type=F32).astype(BF16)
 
     def at(slot, lo=0, hi=HB):
         return terms.at[pl.ds(slot * HB + lo, hi - lo), :]
 
-    def half_right(p, slot):
-        return remote(at(slot, 0, HALF), halves.at[p, 0], h_send.at[p, 0], h_recv.at[p, 0], right)
-
-    def half_left(p, slot):
-        return remote(at(slot, HALF, HB), halves.at[p, 1], h_send.at[p, 1], h_recv.at[p, 1], left)
-
-    def full_right(p, slot):
-        return remote(at(slot), fulls.at[p, 0], f_send.at[p, 0], f_recv.at[p, 0], right)
-
-    def full_left(p, slot):
-        return remote(at(slot), fulls.at[p, 1], f_send.at[p, 1], f_recv.at[p, 1], left)
-
-    def add(lo, hi, more):
-        terms[lo:hi, :] = (terms[lo:hi, :].astype(F32) + more.astype(F32)).astype(BF16)
-
-    slots = ((L0, R0, O0), (L1, R1, O1))
+    def far_half(p, slot, side, lo, hi, peer):
+        return remote(at(slot, lo, hi), halves.at[p, side], h_send.at[p, side], h_recv.at[p, side], peer)
+
+    def near_half(p, slot, side, upper, peer):
+        lo = HALF if upper else 0
+        return remote(
+            at(slot, lo, lo + HALF), fulls.at[p, side, pl.ds(lo, HALF), :],
+            f_send.at[p, side, upper], f_recv.at[p, side, upper], peer,
+        )
+
+    def add(lo, more):
+        rows = slice(lo, lo + HALF)
+        terms[rows, :] = (terms[rows, :].astype(F32) + more.astype(F32)).astype(BF16)
+
     started = []
-    chains = {}
-    for p in (1, 0):
-        left_slot, right_slot, far = slots[p]
-        term(far)
-        hr, hl = half_right(p, far), half_left(p, far)
-        hr.start()
-        hl.start()
-        chains[p] = (hr, hl)
-        started += [hr, hl]
-    for p in (1, 0):
-        left_slot, right_slot, far = slots[p]
-        hr, hl = chains[p]
-        term(left_slot)
-        term(right_slot)
-        hr.wait_recv()
-        add(right_slot * HB, right_slot * HB + HALF, halves[p, 0])
-        fr = full_right(p, right_slot)
-        fr.start()
-        hl.wait_recv()
-        add(left_slot * HB + HALF, left_slot * HB + HB, halves[p, 1])
-        fl = full_left(p, left_slot)
-        fl.start()
-        chains[p] = (fr, fl)
-        started += [fr, fl]
-    term(MIR)
-    term(OWN)
-    for copy in chains[1]:
-        copy.wait_recv()
-    add(MIR * HB, MIR * HB + HB, fulls[1, 0].astype(F32) + fulls[1, 1].astype(F32))
-    to_mirror = remote(at(MIR), mirrored, z_send, z_recv, mirror)
-    to_mirror.start()
-    for copy in chains[0]:
-        copy.wait_recv()
-    to_mirror.wait_recv()
-    total = terms[0:HB, :].astype(F32) + fulls[0, 0].astype(F32)
-    total = total + fulls[0, 1].astype(F32) + mirrored[...].astype(F32)
-    out_ref[...] = total.astype(BF16)
+
+    def begin(copy):
+        copy.start()
+        started.append(copy)
+        return copy
+
+    def send_far(p, slot):
+        return (
+            begin(far_half(p, slot, 0, 0, HALF, right)),
+            begin(far_half(p, slot, 1, HALF, HB, left)),
+        )
+
+    def send_near(p, from_left, from_right, passed):
+        right_hi = begin(near_half(p, from_right, 0, 1, right))
+        left_lo = begin(near_half(p, from_left, 1, 0, left))
+        passed[0].wait_recv()
+        add(from_right * HB, halves[p, 0])
+        right_lo = begin(near_half(p, from_right, 0, 0, right))
+        passed[1].wait_recv()
+        add(from_left * HB + HALF, halves[p, 1])
+        left_hi = begin(near_half(p, from_left, 1, 1, left))
+        return (right_lo, left_lo), (right_hi, left_hi)
+
+    term(0)
+    passed = send_far(1, O1)
+    term(1)
+    low, high = send_near(1, L1, R1, passed)
+    term(2)
+    term(3)
+    passed = send_far(0, O0)
+    mirrors = []
+    for upper, copies in enumerate((low, high)):
+        for copy in copies:
+            copy.wait_recv()
+        rows = slice(upper * HALF, (upper + 1) * HALF)
+        add(MIR * HB + upper * HALF, fulls[1, 0, rows].astype(F32) + fulls[1, 1, rows].astype(F32))
+        mirrors.append(begin(remote(
+            at(MIR, upper * HALF, (upper + 1) * HALF), mirrored.at[rows, :],
+            z_send.at[upper], z_recv.at[upper], mirror,
+        )))
+    term(4)
+    low, high = send_near(0, L0, R0, passed)
+    term(5)
+    for upper, copies in enumerate((low, high)):
+        rows = slice(upper * HALF, (upper + 1) * HALF)
+        for copy in copies:
+            copy.wait_recv()
+        mirrors[upper].wait_recv()
+        total = terms[rows, :].astype(F32) + fulls[0, 0, rows].astype(F32)
+        total = total + fulls[0, 1, rows].astype(F32) + mirrored[rows, :].astype(F32)
+        out_ref[rows, :] = total.astype(BF16)
     for copy in started:
         copy.wait_send()
-    to_mirror.wait_send()
+    for i, (pz, pc) in enumerate(peers):
+        src = pz * 2 + pc
+        remote(o_hbm.at[src], parts.at[src], o_send.at[i], o_recv.at[0, src], ids[i]).wait_send()
 
 
 def combine(o, lse, out_weight):
@@ -441,9 +484,10 @@
     return pl.pallas_call(
         combine_kernel,
         out_shape=jax.ShapeDtypeStruct((HB, D), BF16),
-        in_specs=[hbm, hbm, vmem],
+        in_specs=[hbm, hbm, hbm],
         out_specs=vmem,
         scratch_shapes=[
+            pltpu.VMEM((2 * HD, D), BF16),
             pltpu.VMEM((SRC, ROWS, HD), BF16),
             pltpu.VMEM((SRC, SLOTS, HD), F32),
             pltpu.VMEM((ROWS, 2 * HD), BF16),
@@ -451,11 +495,11 @@
             pltpu.VMEM((2, 2, HALF, D), BF16),
             pltpu.VMEM((2, 2, HB, D), BF16),
             pltpu.VMEM((HB, D), BF16),
-            dma((SRC,)), dma((SRC,)), dma((SRC,)), dma((SRC,)), dma((2,)),
-            dma((2, 2)), dma((2, 2)), dma((2, 2)), dma((2, 2)), dma, dma,
+            dma, dma((SRC,)), dma((len(GROUPS), SRC)), dma((SRC,)), dma((SRC,)), dma((2,)),
+            dma((2, 2)), dma((2, 2)), dma((2, 2, 2)), dma((2, 2, 2)), dma((2,)), dma((2,)),
         ],
         compiler_params=pltpu.CompilerParams(
-            collective_id=1, has_side_effects=True, vmem_limit_bytes=40 << 20
+            collective_id=1, has_side_effects=True, vmem_limit_bytes=60 << 20
         ),
         name="combine",
     )(o.reshape(SRC, ROWS, HD), lse, out_weight)
@@ -463,16 +507,10 @@
 
 def local(hidden_in, norm_gain, qkv_weight, out_weight, block_order):
     y, zl, c, x, zh = place()
-    zero = jnp.zeros((4, 2), jnp.int32)
-    lane = jnp.arange(4, dtype=jnp.int32)[:, None] + zero
-    core = jnp.arange(2, dtype=jnp.int32)[None, :] + zero
-    q_starts = starts_of(block_order, zero + y, lane, core, x, zh)
-    k_starts = starts_of(block_order, lane, zero + zl, core, x, zh)
-    q_order, q_first = sort_chunks(q_starts)
-    k_order, k_first = sort_chunks(k_starts)
-    meta = jnp.stack([q_order, k_order, q_first, k_first])
-
-    mine = starts_of(block_order, y, zl, c, x, zh)
+    starts = starts_of(block_order, y, zl, c, x, zh)
+    order, first = sort_chunks(starts[: 2 * SRC * SLOTS].reshape(2, SRC * SLOTS))
+    meta = jnp.concatenate([order, first], axis=0)
+    mine = starts[2 * SRC * SLOTS :]
     position = (mine[:, None] + jnp.arange(HB, dtype=jnp.int32)[None, :]).reshape(-1)
     inv_freq = 10000.0 ** (-(jnp.arange(HD // 2, dtype=F32) * 2.0 / HD))
     angle = position.astype(F32)[:, None] * inv_freq[None, :]

time: 194 us -> 148 us (0.76)
  the two profiles are of different devices: /device:TPU:1 before, /device:TPU:9 now
where the time goes in v2:
time: 148 us
  Pallas kernels  141 us (95%)
  other arithmetic  5.22 us (4%)
  local copies, waits for them, and re-layouts  2.04 us (1%)
    pallas_call x1, Pallas kernels, combine(): pl.pallas_call(combine_kernel, out_shape=jax.ShapeDtypeStruct((HB, D), BF...  58.3 us
    pallas_call x1, Pallas kernels, project(): pl.pallas_call(project_kernel, out_shape=(jax.ShapeDtypeStruct((SRC, ROWS...  54.9 us
    pallas_call x1, Pallas kernels, attend(): pl.pallas_call(attend_kernel, out_shape=(jax.ShapeDtypeStruct((chunks, HB...  27.4 us

profile of v2, /device:TPU:9, one launch (start us, length us, event | category | flops | bytes accessed | tf_op | source)
XLA Modules:
  0.0 147.8 jit_solution(515229777035473374)
XLA Ops:
  0.0 0.8 and_add_fusion
  0.8 0.8 select_reduce_fusion
  1.6 0.7 multiply_add_fusion
  2.3 0.1 lt.32
  2.4 0.1 convert_reduce_fusion
  2.5 0.2 select_reduce_fusion.2
  2.6 0.6 pad_add_fusion.meta
  3.2 0.1 add_convert_fusion
  3.3 0.1 convert_element_type.15
  3.4 1.0 fusion
  4.4 1.0 pad_maximum_fusion
  5.4 54.9 %project.1 = (bf16[8,512,128]{2,1,0:T(8,128)(2,1)}, bf16[8,512,256]{2,1,0:T(8,128)(2,1)}) custom-call(bf16[64,4096]{1,0:T(8,128)(2,1)} %hid.1, f32[1,4096]{1,0:T(1,128)} %bitcast.9, bf16[3,4096,256]{2,1,0:T(8,128)(2,1)} %bitcast.5, f32[512,128]{1,0:T(8,128)} %get-tuple-element.18.cos, f32[512,128]{1,0:T(8,128)} %get-tuple-element.19.sin), custom_call_target="tpu_custom_call" | custom-call | tf_op jit(solution)/shard_map/project/pallas_call | solution.py:217
  60.3 27.4 %attend.1 = (bf16[64,64,128]{2,1,0:T(8,128)(2,1)}, f32[8,8,128]{2,1,0:T(8,128)}) custom-call(s32[4,64]{1,0:T(4,128)} %pad_add_fusion.meta, bf16[64,64,128]{2,1,0:T(8,128)(2,1)} %bitcast.8, bf16[64,64,256]{2,1,0:T(8,128)(2,1)} %bitcast.6), custom_call_target="tpu_custom_call" | custom-call | tf_op jit(solution)/shard_map/attend/pallas_call | solution.py:316
  87.7 58.3 %combine.1 = bf16[64,4096]{1,0:T(8,128)(2,1)} custom-call(bf16[8,512,128]{2,1,0:T(8,128)(2,1)} %bitcast.7, f32[8,8,128]{2,1,0:T(8,128)} %get-tuple-element.12.lse_in, bf16[256,4096]{1,0:T(8,128)(2,1)} %w_hbm.1), custom_call_target="tpu_custom_call" | custom-call | tf_op jit(solution)/shard_map/combine/pallas_call | solution.py:484
  146.0 1.9 %copy.15 = bf16[64,4096]{1,0:T(8,128)(2,1)} copy(bf16[64,4096]{1,0:T(8,128)(2,1)} %combine.1) | data formatting | bytes 1048576
  (3 shorter events, 0.0 us)

commit v3 on v2

v3 whole, which is shorter than its diff:
```python
import math

import jax
import jax.numpy as jnp
import numpy as np
from jax import lax
from jax.experimental import pallas as pl
from jax.experimental.pallas import tpu as pltpu
from jax.sharding import PartitionSpec as P

HD = 128
BLK = 128
D = 4096
SEQ = 16384
HB = 64
SLOTS = 8
ROWS = HB * SLOTS
SRC = 8
ALL = SRC * ROWS
HALF = HB // 2
TQ = SRC * HB
TK = 1024
MESH = pl.DeviceIdType.MESH
F32 = jnp.float32
BF16 = jnp.bfloat16

O1, L1, R1, MIR, O0, L0, R0, OWN = range(8)
CHUNKS = ((1, 2), (1, -1), (1, 1), (1, 0), (0, 2), (0, -1), (0, 1), (0, 0))
SCALE = math.log2(math.e) / HD**0.5
OTHERS = [(d, e) for d in range(4) for e in range(2)][1:]


def place():
    s = lax.axis_index("seq")
    t = lax.axis_index("tp")
    return s // 8, (s // 2) % 4, s % 2, t // 2, t % 2


def device(y, zl, c, x, zh):
    return ((y * 4 + zl) * 2 + c, x * 2 + zh)


def other_core(c, e):
    return 1 - c if e else c


def start_of(order, slot, y, zl, c, x, zh):
    mirrored, shift = CHUNKS[slot]
    if mirrored:
        zl, zh = 3 - zl, 1 - zh
    block = ((y * 4 + zl) * 2 + c) * (ROWS // BLK) + (x + shift + 4) % 4
    return order[block] * BLK + zh * HB


def tables():
    frequency = 10000.0 ** (-(np.arange(HD) % (HD // 2)) * 2.0 / HD)
    starts = np.arange(SEQ // HB)[:, None] * float(HB) * frequency[None, :]
    rows = np.arange(HB)[:, None] * frequency[None, :]
    made = [np.cos(starts), np.sin(starts), np.cos(rows), np.sin(rows)]
    return [jnp.asarray(t.astype(np.float32)) for t in made]


def greet(peers):
    barrier = pltpu.get_barrier_semaphore()
    for peer in peers:
        pl.semaphore_signal(barrier, inc=1, device_id=peer, device_id_type=MESH)
    return barrier


def remote(src, dst, send, recv, peer):
    return pltpu.make_async_remote_copy(
        src_ref=src, dst_ref=dst, send_sem=send, recv_sem=recv, device_id=peer, device_id_type=MESH
    )


def project_kernel(
    order, hid, gain, w_hbm, cos_start, sin_start, cos_row, sin_row, q_out, kv_out,
    rows, cos, sin, wv, qs, kvs, w_sem, x_send, x_recv, z_send, z_recv,
    kv_send, kv_recv, q_send, q_recv, own_sem,
):
    y, zl, c, x, zh = place()
    right = device(y, zl, c, (x + 1) % 4, zh)
    left = device(y, zl, c, (x + 3) % 4, zh)
    mirror = device(y, 3 - zl, c, x, 1 - zh)
    kv_peers = [((y + d) % 4, other_core(c, e)) for d, e in OTHERS]
    q_peers = [((zl + d) % 4, other_core(c, e)) for d, e in OTHERS]
    kv_ids = [device(py, zl, pc, x, zh) for py, pc in kv_peers]
    q_ids = [device(y, pz, pc, x, zh) for pz, pc in q_peers]
    peers = [right, left, mirror] + kv_ids + q_ids[1:]
    barrier = greet(peers)
    w_copy = pltpu.make_async_copy(w_hbm, wv, w_sem)
    w_copy.start()

    floats = hid[...].astype(F32)
    scale = lax.rsqrt(jnp.mean(floats * floats, axis=-1, keepdims=True) + 1e-05)
    rows[OWN * HB : (OWN + 1) * HB, :] = (floats * scale * gain[...]).astype(BF16)
    first_half = lax.broadcasted_iota(jnp.int32, (1, HD), 1) < HD // 2
    for slot in range(SLOTS):
        start = start_of(order, slot, y, zl, c, x, zh) // HB
        cs, sn = cos_start[pl.ds(start, 1), :], sin_start[pl.ds(start, 1), :]
        lo, hi = slot * HB, (slot + 1) * HB
        cos[lo:hi, :] = cs * cos_row[...] - sn * sin_row[...]
        sine = sn * cos_row[...] + cs * sin_row[...]
        sin[lo:hi, :] = jnp.where(first_half, -sine, sine)
    pl.semaphore_wait(barrier, len(peers))

    def at(slot, lo=0, hi=HB):
        return rows.at[pl.ds(slot * HB + lo, hi - lo), :]

    def step(p, kind, src, dst, lo, hi, peer):
        return remote(at(src, lo, hi), at(dst, lo, hi), x_send.at[p, kind], x_recv.at[p, kind], peer)

    def ring(p, src, from_left, from_right, far):
        return (
            step(p, 0, src, from_left, 0, HALF, right),
            step(p, 1, src, from_right, HALF, HB, left),
            step(p, 2, src, from_left, HALF, HB, right),
            step(p, 3, src, from_right, 0, HALF, left),
            step(p, 4, from_left, far, 0, HALF, right),
            step(p, 5, from_right, far, HALF, HB, left),
        )

    mirror_lo = remote(at(OWN, 0, HALF), at(MIR, 0, HALF), z_send.at[0], z_recv.at[0], mirror)
    mirror_hi = remote(at(OWN, HALF, HB), at(MIR, HALF, HB), z_send.at[1], z_recv.at[1], mirror)
    near = ring(0, OWN, L0, R0, O0)
    far = ring(1, MIR, L1, R1, O1)

    mirror_lo.start()
    mirror_hi.start()
    for copy in near[:4]:
        copy.start()
    mine = y * 2 + c
    mine_q = zl * 2 + c

    def part(ref, lo, hi, *index):
        return ref.at[(*index, pl.ds(lo, hi - lo), slice(None))]

    def work(first, last):
        lo, hi = first * HB, last * HB
        chunk = rows[lo:hi, :]
        cs, sn = cos[lo:hi, :], sin[lo:hi, :]
        q = jnp.dot(chunk, wv[0], preferred_element_type=F32)
        k = jnp.dot(chunk, wv[1], preferred_element_type=F32)
        v = jnp.dot(chunk, wv[2], preferred_element_type=F32)
        for h in range(2):
            lane = slice(h * HD, (h + 1) * HD)
            for out, by, t in ((qs, SCALE, q[:, lane]), (kvs, 1.0, k[:, lane])):
                turned = t * cs + pltpu.roll(t, HD // 2, 1) * sn
                out[h, lo:hi, 0:HD] = (turned * by).astype(BF16)
            kvs[h, lo:hi, HD : 2 * HD] = v[:, lane].astype(BF16)
        for i, (py, pc) in enumerate(kv_peers):
            remote(
                part(kvs, lo, hi, pc), part(kv_out, lo, hi, mine),
                kv_send.at[i], kv_recv.at[mine], kv_ids[i],
            ).start()
        for i, (pz, pc) in enumerate(q_peers):
            remote(
                part(qs, lo, hi, pc), part(q_out, lo, hi, mine_q),
                q_send.at[i], q_recv.at[mine_q], q_ids[i],
            ).start()

    w_copy.wait()
    work(OWN, OWN + 1)
    near[0].wait_recv()
    near[4].start()
    near[1].wait_recv()
    near[5].start()
    near[2].wait_recv()
    near[3].wait_recv()
    work(L0, R0 + 1)
    mirror_lo.wait_recv()
    far[0].start()
    far[3].start()
    near[4].wait_recv()
    near[5].wait_recv()
    work(O0, O0 + 1)
    mirror_hi.wait_recv()
    far[1].start()
    far[2].start()
    work(MIR, MIR + 1)
    far[0].wait_recv()
    far[4].start()
    far[1].wait_recv()
    far[5].start()
    far[2].wait_recv()
    far[3].wait_recv()
    work(L1, R1 + 1)
    far[4].wait_recv()
    far[5].wait_recv()
    work(O1, O1 + 1)
    own_kv = pltpu.make_async_copy(kvs.at[c], kv_out.at[mine], own_sem.at[0])
    own_q = pltpu.make_async_copy(qs.at[c], q_out.at[mine_q], own_sem.at[1])
    own_kv.start()
    own_q.start()
    for copy in (mirror_lo, mirror_hi, *near, *far):
        copy.wait_send()
    for i, (py, pc) in enumerate(kv_peers):
        src = py * 2 + pc
        done = remote(kvs.at[pc], kv_out.at[src], kv_send.at[i], kv_recv.at[src], kv_ids[i])
        done.wait_send()
        done.wait_recv()
    for i, (pz, pc) in enumerate(q_peers):
        src = pz * 2 + pc
        done = remote(qs.at[pc], q_out.at[src], q_send.at[i], q_recv.at[src], q_ids[i])
        done.wait_send()
        done.wait_recv()
    own_kv.wait()
    own_q.wait()


def project(block_order, hidden_in, norm_gain, weight):
    vmem = pl.BlockSpec(memory_space=pltpu.VMEM)
    hbm = pl.BlockSpec(memory_space=pl.ANY)
    dma = pltpu.SemaphoreType.DMA
    return pl.pallas_call(
        project_kernel,
        out_shape=(
            jax.ShapeDtypeStruct((SRC, ROWS, HD), BF16),
            jax.ShapeDtypeStruct((SRC, ROWS, 2 * HD), BF16),
        ),
        in_specs=[pl.BlockSpec(memory_space=pltpu.SMEM), vmem, vmem, hbm, vmem, vmem, vmem, vmem],
        out_specs=(hbm, hbm),
        scratch_shapes=[
            pltpu.VMEM((ROWS, D), BF16),
            pltpu.VMEM((ROWS, HD), F32),
            pltpu.VMEM((ROWS, HD), F32),
            pltpu.VMEM((3, D, 2 * HD), BF16),
            pltpu.VMEM((2, ROWS, HD), BF16),
            pltpu.VMEM((2, ROWS, 2 * HD), BF16),
            dma, dma((2, 6)), dma((2, 6)), dma((2,)), dma((2,)),
            dma((SRC,)), dma((SRC,)), dma((SRC,)), dma((SRC,)), dma((2,)),
        ],
        compiler_params=pltpu.CompilerParams(
            collective_id=0, has_side_effects=True, vmem_limit_bytes=60 << 20
        ),
        name="project",
    )(block_order, hidden_in, norm_gain, weight, *tables())


def attend_kernel(
    order, q_hbm, kv_hbm, w_hbm, out_ref,
    q_ref, kv_ref, w_ref, scores, top, sums, qpos, kpos, o_mine, l_mine, parts, lses,
    ctx, terms, halves, fulls, mirrored,
    in_sem, o_send, o_recv, l_send, l_recv, h_send, h_recv, f_send, f_recv, z_send, z_recv,
):
    y, zl, c, x, zh = place()
    right = device(y, zl, c, (x + 1) % 4, zh)
    left = device(y, zl, c, (x + 3) % 4, zh)
    mirror = device(y, 3 - zl, c, x, 1 - zh)
    peers = [((zl + d) % 4, other_core(c, e)) for d, e in OTHERS]
    ids = [device(y, pz, pc, x, zh) for pz, pc in peers]
    mine = zl * 2 + c
    barrier = greet([right, left, mirror] + ids)
    loads = [
        pltpu.make_async_copy(src, dst, in_sem.at[i])
        for i, (src, dst) in enumerate(((q_hbm, q_ref), (kv_hbm, kv_ref), (w_hbm, w_ref)))
    ]
    for load in loads:
        load.start()

    lane = lax.broadcasted_iota(jnp.int32, (1, HD), 1)
    row = lax.broadcasted_iota(jnp.int32, (HB, HD), 0)
    for src in range(SRC):
        starts = [start_of(order, slot, src // 2, zl, src % 2, x, zh) for slot in range(SLOTS)]
        for u in range(SLOTS // 2):
            kpos[src * (SLOTS // 2) + u] = jnp.where(
                lane < HB, starts[2 * u] + lane, starts[2 * u + 1] + lane - HB
            )
        for slot in range(SLOTS):
            qpos[slot, src * HB : (src + 1) * HB, :] = row + start_of(
                order, slot, y, src // 2, src % 2, x, zh
            )
    diagonal = lax.broadcasted_iota(jnp.int32, (HD, HD), 0) == lax.broadcasted_iota(
        jnp.int32, (HD, HD), 1
    )
    per = TK // HD
    for load in loads:
        load.wait()
    pl.semaphore_wait(barrier, len(ids) + 3)

    def attend_chunk(t):
        at = pl.ds(pl.multiple_of(t * HB, HB), HB)
        q = q_ref[:, at, :].reshape(TQ, HD)
        top[...] = jnp.full((TQ, HD), -1e29, F32)
        sums[...] = jnp.zeros((TQ, HD), F32)
        for j in range(ALL // TK):
            keys = kv_ref[j * TK : (j + 1) * TK, 0:HD]
            s = lax.dot_general(q, keys, (((1,), (1,)), ((), ())), preferred_element_type=F32)
            best = top[...]
            for u in range(per):
                keep = kpos[j * per + u] <= qpos[t]
                kept = jnp.where(keep, s[:, u * HD : (u + 1) * HD], -1e30)
                scores[j * per + u] = kept
                best = jnp.maximum(best, kept)
            top[...] = best
        best = jnp.broadcast_to(jnp.max(top[...], axis=1, keepdims=True), (TQ, HD))
        acc = jnp.zeros((TQ, HD), F32)
        for j in range(ALL // TK):
            weight = [jnp.exp2(scores[j * per + u] - best) for u in range(per)]
            total = sums[...]
            for part in weight:
                total = total + part
            sums[...] = total
            weight = jnp.concatenate([part.astype(BF16) for part in weight], axis=1)
            values = kv_ref[j * TK : (j + 1) * TK, HD : 2 * HD]
            acc = acc + jnp.dot(weight, values, preferred_element_type=F32)
        total = jnp.broadcast_to(jnp.sum(sums[...], axis=1, keepdims=True), (TQ, HD))
        some = total > 0
        total = jnp.where(some, total, 1.0)
        o_mine[t] = (acc / total).astype(BF16).reshape(SRC, HB, HD)
        lse = jnp.where(some, best + jnp.log2(total), -1e30)
        for u in range(SRC // 2):
            block = lse[u * HD : (u + 1) * HD, :]
            line = jnp.sum(jnp.where(diagonal, block, 0.0), axis=0, keepdims=True)
            l_mine[t, 2 * u, 0:1, :] = line
            l_mine[t, 2 * u + 1, 0:1, :] = pltpu.roll(line, HB, 1)
        parts[t, mine] = o_mine[t, mine]
        lses[t, mine] = l_mine[t, mine]
        for i, (pz, pc) in enumerate(peers):
            to = pz * 2 + pc
            remote(
                l_mine.at[t, to], lses.at[t, mine], l_send.at[i], l_recv.at[t, mine], ids[i]
            ).start()
            remote(
                o_mine.at[t, to], parts.at[t, mine], o_send.at[i], o_recv.at[t, mine], ids[i]
            ).start()

    def term(t):
        for i, (pz, pc) in enumerate(peers):
            src = pz * 2 + pc
            remote(
                l_mine.at[t, src], lses.at[t, src], l_send.at[i], l_recv.at[t, src], ids[i]
            ).wait_recv()
            remote(
                o_mine.at[t, src], parts.at[t, src], o_send.at[i], o_recv.at[t, src], ids[i]
            ).wait_recv()
        stats = jnp.concatenate([lses[t, src, 0:1, :] for src in range(SRC)], axis=0)
        stats = jnp.concatenate([stats] * (HD // SRC), axis=0).T
        for h in range(2):
            cols = [stats[0:HB, z * 2 + h : z * 2 + h + 1] for z in range(4)]
            best = jnp.maximum(jnp.maximum(cols[0], cols[1]), jnp.maximum(cols[2], cols[3]))
            shares = [jnp.exp2(col - best) for col in cols]
            total = shares[0] + shares[1] + shares[2] + shares[3]
            mixed = jnp.zeros((HB, HD), F32)
            for z in range(4):
                mixed += (shares[z] / total) * parts[t, z * 2 + h].astype(F32)
            ctx[:, h * HD : (h + 1) * HD] = mixed.astype(BF16)
        at = pl.ds(pl.multiple_of(t * HB, HB), HB)
        terms[at, :] = jnp.dot(ctx[...], w_ref[...], preferred_element_type=F32).astype(BF16)

    def cols(v):
        return pl.ds(v * (D // 2), D // 2)

    def at(slot, lo, v):
        return terms.at[pl.ds(slot * HB + lo, HALF), cols(v)]

    def far(p, slot, side, v):
        return remote(
            at(slot, side * HALF, v), halves.at[p, side, :, cols(v)],
            h_send.at[p, side, v], h_recv.at[p, side, v], left if side else right,
        )

    def near(p, slot, side, upper, v):
        return remote(
            at(slot, upper * HALF, v), fulls.at[p, side, pl.ds(upper * HALF, HALF), cols(v)],
            f_send.at[p, side, upper, v], f_recv.at[p, side, upper, v], left if side else right,
        )

    def over(upper, v):
        return remote(
            at(MIR, upper * HALF, v), mirrored.at[pl.ds(upper * HALF, HALF), cols(v)],
            z_send.at[upper, v], z_recv.at[upper, v], mirror,
        )

    fars, nears = (O0, O1), ((R0, L0), (R1, L1))

    def add(lo, v, *more):
        rows, columns = slice(lo, lo + HALF), slice(v * (D // 2), (v + 1) * (D // 2))
        total = terms[rows, columns].astype(F32)
        for ref in more:
            total = total + ref[:, columns].astype(F32)
        return total

    def store(lo, v, total):
        terms[lo : lo + HALF, v * (D // 2) : (v + 1) * (D // 2)] = total.astype(BF16)

    def send_far(p):
        for v in range(2):
            for side in range(2):
                far(p, fars[p], side, v).start()

    def send_near(p, side):
        slot = nears[p][side]
        lo = slot * HB + side * HALF
        for v in range(2):
            near(p, slot, side, 1 - side, v).start()
            far(p, fars[p], side, v).wait_recv()
            store(lo, v, add(lo, v, halves.at[p, side]))
            near(p, slot, side, side, v).start()

    def send_over(v):
        for upper in range(2):
            for side in range(2):
                near(1, nears[1][side], side, upper, v).wait_recv()
            lo = MIR * HB + upper * HALF
            rows = pl.ds(upper * HALF, HALF)
            store(lo, v, add(lo, v, fulls.at[1, 0, rows], fulls.at[1, 1, rows]))
            over(upper, v).start()

    @pl.loop(0, SLOTS)
    def _(t):
        attend_chunk(t)
        pl.when(t > 0)(lambda: term(t - 1))

        @pl.when(t == O1 + 1)
        def _():
            send_far(1)

        @pl.when(t == L1 + 1)
        def _():
            send_near(1, 1)

        @pl.when(t == R1 + 1)
        def _():
            send_near(1, 0)

        @pl.when(t == O0 + 1)
        def _():
            send_far(0)
            send_over(0)

        @pl.when(t == L0 + 1)
        def _():
            send_over(1)
            send_near(0, 1)

        @pl.when(t == R0 + 1)
        def _():
            send_near(0, 0)

    term(OWN)
    for v in range(2):
        for upper in range(2):
            for side in range(2):
                near(0, nears[0][side], side, upper, v).wait_recv()
            over(upper, v).wait_recv()
            rows = pl.ds(upper * HALF, HALF)
            total = add(
                OWN * HB + upper * HALF, v, fulls.at[0, 0, rows], fulls.at[0, 1, rows], mirrored.at[rows]
            )
            out_ref[rows, v * (D // 2) : (v + 1) * (D // 2)] = total.astype(BF16)
    for v in range(2):
        for p in range(2):
            for side in range(2):
                far(p, fars[p], side, v).wait_send()
                for upper in range(2):
                    near(p, nears[p][side], side, upper, v).wait_send()
        for upper in range(2):
            over(upper, v).wait_send()
    for i, (pz, pc) in enumerate(peers):
        src = pz * 2 + pc
        remote(l_mine.at[:, src], lses.at[:, src], l_send.at[i], l_recv.at[0, src], ids[i]).wait_send()
        remote(o_mine.at[:, src], parts.at[:, src], o_send.at[i], o_recv.at[0, src], ids[i]).wait_send()


def attend(block_order, q, kv, out_weight):
    vmem = pl.BlockSpec(memory_space=pltpu.VMEM)
    hbm = pl.BlockSpec(memory_space=pl.ANY)
    dma = pltpu.SemaphoreType.DMA
    return pl.pallas_call(
        attend_kernel,
        out_shape=jax.ShapeDtypeStruct((HB, D), BF16),
        in_specs=[pl.BlockSpec(memory_space=pltpu.SMEM), hbm, hbm, hbm],
        out_specs=vmem,
        scratch_shapes=[
            pltpu.VMEM((SRC, ROWS, HD), BF16),
            pltpu.VMEM((ALL, 2 * HD), BF16),
            pltpu.VMEM((2 * HD, D), BF16),
            pltpu.VMEM((ALL // HD, TQ, HD), F32),
            pltpu.VMEM((TQ, HD), F32),
            pltpu.VMEM((TQ, HD), F32),
            pltpu.VMEM((SLOTS, TQ, HD), jnp.int32),
            pltpu.VMEM((ALL // HD, 1, HD), jnp.int32),
            pltpu.VMEM((SLOTS, SRC, HB, HD), BF16),
            pltpu.VMEM((SLOTS, SRC, 8, HD), F32),
            pltpu.VMEM((SLOTS, SRC, HB, HD), BF16),
            pltpu.VMEM((SLOTS, SRC, 8, HD), F32),
            pltpu.VMEM((HB, 2 * HD), BF16),
            pltpu.VMEM((ROWS, D), BF16),
            pltpu.VMEM((2, 2, HALF, D), BF16),
            pltpu.VMEM((2, 2, HB, D), BF16),
            pltpu.VMEM((HB, D), BF16),
            dma((3,)),
            dma((SRC,)), dma((SLOTS, SRC)), dma((SRC,)), dma((SLOTS, SRC)),
            dma((2, 2, 2)), dma((2, 2, 2)), dma((2, 2, 2, 2)), dma((2, 2, 2, 2)),
            dma((2, 2)), dma((2, 2)),
        ],
        compiler_params=pltpu.CompilerParams(
            collective_id=1, has_side_effects=True, vmem_limit_bytes=58 << 20
        ),
        name="attend",
    )(block_order, q, kv.reshape(ALL, 2 * HD), out_weight)


def local(hidden_in, norm_gain, qkv_weight, out_weight, block_order):
    weight = jnp.transpose(qkv_weight, (1, 0, 2))
    q, kv = project(block_order, hidden_in, norm_gain[None, :], weight)
    return attend(block_order, q, kv, out_weight)


def solution(mesh):
    in_specs = (P(("seq", "tp"), None), P(), P(None, None, "tp"), P("tp", None), P())
    out_specs = P(("seq", "tp"), None)
    return jax.shard_map(local, mesh=mesh, in_specs=in_specs, out_specs=out_specs, check_vma=False)
```

time: 148 us -> 138 us (0.932)
  the two profiles are of different devices: /device:TPU:9 before, /device:TPU:33 now
where the time goes in v3:
time: 138 us; the launch traced here: 135 us
  Pallas kernels  133 us (96%)
  local copies, waits for them, and re-layouts  1.87 us (1%)
    pallas_call x1, Pallas kernels, attend(): pl.pallas_call(attend_kernel, out_shape=jax.ShapeDtypeStruct((HB, D), BF1...  79.5 us
    pallas_call x1, Pallas kernels, project(): pl.pallas_call(project_kernel, out_shape=(jax.ShapeDtypeStruct((SRC, ROWS...  53.8 us

profile of v3, /device:TPU:33, one launch (start us, length us, event | category | flops | bytes accessed | tf_op | source)
XLA Modules:
  0.0 135.3 jit_solution(15233253822657712239)
XLA Ops:
  0.0 53.8 %project.1 = (bf16[8,512,128]{2,1,0:T(8,128)(2,1)}, bf16[8,512,256]{2,1,0:T(8,128)(2,1)}) custom-call(s32[128]{0:T(128)} %order.3, bf16[64,4096]{1,0:T(8,128)(2,1)} %hid.1, f32[1,4096]{1,0:T(1,128)} %bitcast.5, bf16[3,4096,256]{2,1,0:T(8,128)(2,1)} %bitcast.3, f32[256,128]{1,0:T(8,128)} %constant.8.clone.cos_start, f32[256,128]{1,0:T(8,128)} %constant.9.clone.sin_start, ...), custom_call_target="tpu_custom_call" | custom-call | tf_op jit(solution)/shard_map/project/pallas_call | solution.py:215
  53.8 79.5 %attend.1 = bf16[64,4096]{1,0:T(8,128)(2,1)} custom-call(s32[128]{0:T(128)} %order.3, bf16[8,512,128]{2,1,0:T(8,128)(2,1)} %get-tuple-element.7.q_hbm, bf16[4096,256]{1,0:T(8,128)(2,1)} %bitcast.4, bf16[256,4096]{1,0:T(8,128)(2,1)} %w_hbm.1), custom_call_target="tpu_custom_call" | custom-call | tf_op jit(solution)/shard_map/attend/pallas_call | solution.py:470
  133.4 1.9 %copy.11 = bf16[64,4096]{1,0:T(8,128)(2,1)} copy(bf16[64,4096]{1,0:T(8,128)(2,1)} %attend.1) | data formatting | bytes 1048576

commit v4 on v3

--- a/solution.py
+++ b/solution.py
@@ -19,7 +19,7 @@
 ALL = SRC * ROWS
 HALF = HB // 2
 TQ = SRC * HB
-TK = 1024
+TK = 4096
 MESH = pl.DeviceIdType.MESH
 F32 = jnp.float32
 BF16 = jnp.bfloat16
@@ -239,7 +239,7 @@
 
 def attend_kernel(
     order, q_hbm, kv_hbm, w_hbm, out_ref,
-    q_ref, kv_ref, w_ref, scores, top, sums, qpos, kpos, o_mine, l_mine, parts, lses,
+    q_ref, kv_ref, w_ref, values, scores_a, scores_b, top_a, top_b, summed, qpos, kpos, o_mine, l_mine, parts, lses,
     ctx, terms, halves, fulls, mirrored,
     in_sem, o_send, o_recv, l_send, l_recv, h_send, h_recv, f_send, f_recv, z_send, z_recv,
 ):
@@ -274,41 +274,53 @@
         jnp.int32, (HD, HD), 1
     )
     per = TK // HD
+    values[:, HD:] = jnp.ones((ALL, HD), BF16)
     for load in loads:
         load.wait()
+    values[:, :HD] = kv_ref[:, HD:]
     pl.semaphore_wait(barrier, len(ids) + 3)
 
-    def attend_chunk(t):
+    def score_tile(t, j, scores, top):
         at = pl.ds(pl.multiple_of(t * HB, HB), HB)
         q = q_ref[:, at, :].reshape(TQ, HD)
+        keys = kv_ref[pl.ds(pl.multiple_of(j * TK, TK), TK), 0:HD]
+        s = lax.dot_general(q, keys, (((1,), (1,)), ((), ())), preferred_element_type=F32)
+        best = top[...]
+        for u in range(per):
+            keep = kpos[j * per + u] <= qpos[t]
+            kept = jnp.where(keep, s[:, u * HD : (u + 1) * HD], -1e30)
+            scores[j * per + u] = kept
+            best = jnp.maximum(best, kept)
+        top[...] = best
+
+    def weigh_tile(j, scores, top):
+        best = top[...]
+        weight = [jnp.exp2(scores[j * per + u] - best).astype(BF16) for u in range(per)]
+        at = pl.ds(pl.multiple_of(j * TK, TK), TK)
+        summed[...] += jnp.dot(
+            jnp.concatenate(weight, axis=1), values[at, :], preferred_element_type=F32
+        )
+
+    def clear(top):
         top[...] = jnp.full((TQ, HD), -1e29, F32)
-        sums[...] = jnp.zeros((TQ, HD), F32)
-        for j in range(ALL // TK):
-            keys = kv_ref[j * TK : (j + 1) * TK, 0:HD]
-            s = lax.dot_general(q, keys, (((1,), (1,)), ((), ())), preferred_element_type=F32)
-            best = top[...]
-            for u in range(per):
-                keep = kpos[j * per + u] <= qpos[t]
-                kept = jnp.where(keep, s[:, u * HD : (u + 1) * HD], -1e30)
-                scores[j * per + u] = kept
-                best = jnp.maximum(best, kept)
-            top[...] = best
-        best = jnp.broadcast_to(jnp.max(top[...], axis=1, keepdims=True), (TQ, HD))
-        acc = jnp.zeros((TQ, HD), F32)
-        for j in range(ALL // TK):
-            weight = [jnp.exp2(scores[j * per + u] - best) for u in range(per)]
-            total = sums[...]
-            for part in weight:
-                total = total + part
-            sums[...] = total
-            weight = jnp.concatenate([part.astype(BF16) for part in weight], axis=1)
-            values = kv_ref[j * TK : (j + 1) * TK, HD : 2 * HD]
-            acc = acc + jnp.dot(weight, values, preferred_element_type=F32)
-        total = jnp.broadcast_to(jnp.sum(sums[...], axis=1, keepdims=True), (TQ, HD))
+
+    def attend_chunk(t, scores, top, next_scores=None, next_top=None):
+        top[...] = jnp.broadcast_to(jnp.max(top[...], axis=1, keepdims=True), (TQ, HD))
+        summed[...] = jnp.zeros((TQ, 2 * HD), F32)
+        if next_top is not None:
+            clear(next_top)
+
+        @pl.loop(0, ALL // TK)
+        def _(j):
+            if next_top is not None:
+                score_tile(t + 1, j, next_scores, next_top)
+            weigh_tile(j, scores, top)
+
+        total = summed[:, HD:]
         some = total > 0
         total = jnp.where(some, total, 1.0)
-        o_mine[t] = (acc / total).astype(BF16).reshape(SRC, HB, HD)
-        lse = jnp.where(some, best + jnp.log2(total), -1e30)
+        o_mine[t] = (summed[:, :HD] / total).astype(BF16).reshape(SRC, HB, HD)
+        lse = jnp.where(some, top[...] + jnp.log2(total), -1e30)
         for u in range(SRC // 2):
             block = lse[u * HD : (u + 1) * HD, :]
             line = jnp.sum(jnp.where(diagonal, block, 0.0), axis=0, keepdims=True)
@@ -407,9 +419,7 @@
             store(lo, v, add(lo, v, fulls.at[1, 0, rows], fulls.at[1, 1, rows]))
             over(upper, v).start()
 
-    @pl.loop(0, SLOTS)
-    def _(t):
-        attend_chunk(t)
+    def ring(t):
         pl.when(t > 0)(lambda: term(t - 1))
 
         @pl.when(t == O1 + 1)
@@ -434,10 +444,21 @@
             send_over(1)
             send_near(0, 1)
 
-        @pl.when(t == R0 + 1)
-        def _():
-            send_near(0, 0)
-
+    clear(top_a)
+    pl.loop(0, ALL // TK)(lambda j: score_tile(0, j, scores_a, top_a))
+
+    @pl.loop(0, SLOTS // 2 - 1)
+    def _(i):
+        attend_chunk(2 * i, scores_a, top_a, scores_b, top_b)
+        ring(2 * i)
+        attend_chunk(2 * i + 1, scores_b, top_b, scores_a, top_a)
+        ring(2 * i + 1)
+
+    attend_chunk(SLOTS - 2, scores_a, top_a, scores_b, top_b)
+    ring(SLOTS - 2)
+    attend_chunk(SLOTS - 1, scores_b, top_b)
+    term(R0)
+    send_near(0, 0)
     term(OWN)
     for v in range(2):
         for upper in range(2):
@@ -476,9 +497,12 @@
             pltpu.VMEM((SRC, ROWS, HD), BF16),
             pltpu.VMEM((ALL, 2 * HD), BF16),
             pltpu.VMEM((2 * HD, D), BF16),
+            pltpu.VMEM((ALL, 2 * HD), BF16),
+            pltpu.VMEM((ALL // HD, TQ, HD), F32),
             pltpu.VMEM((ALL // HD, TQ, HD), F32),
             pltpu.VMEM((TQ, HD), F32),
             pltpu.VMEM((TQ, HD), F32),
+            pltpu.VMEM((TQ, 2 * HD), F32),
             pltpu.VMEM((SLOTS, TQ, HD), jnp.int32),
             pltpu.VMEM((ALL // HD, 1, HD), jnp.int32),
             pltpu.VMEM((SLOTS, SRC, HB, HD), BF16),
@@ -496,7 +520,7 @@
             dma((2, 2)), dma((2, 2)),
         ],
         compiler_params=pltpu.CompilerParams(
-            collective_id=1, has_side_effects=True, vmem_limit_bytes=58 << 20
+            collective_id=1, has_side_effects=True, vmem_limit_bytes=56 << 20
         ),
         name="attend",
     )(block_order, q, kv.reshape(ALL, 2 * HD), out_weight)

time: 138 us -> 123 us (0.89)
  Pallas kernels: 133 us -> 119 us
    pallas_call x1, Pallas kernels: 79.5 us -> 65 us  [attend(): pl.pallas_call(attend_kernel, out_shape=jax.ShapeDtypeStruct((HB, D), BF1...]
where the time goes in v4:
time: 123 us; the launch traced here: 121 us
  Pallas kernels  119 us (97%)
  local copies, waits for them, and re-layouts  1.87 us (2%)
    pallas_call x1, Pallas kernels, attend(): pl.pallas_call(attend_kernel, out_shape=jax.ShapeDtypeStruct((HB, D), BF1...  65 us
    pallas_call x1, Pallas kernels, project(): pl.pallas_call(project_kernel, out_shape=(jax.ShapeDtypeStruct((SRC, ROWS...  53.8 us

profile of v4, /device:TPU:33, one launch (start us, length us, event | category | flops | bytes accessed | tf_op | source)
XLA Modules:
  0.0 120.7 jit_solution(14338540261881598277)
XLA Ops:
  0.0 53.8 %project.1 = (bf16[8,512,128]{2,1,0:T(8,128)(2,1)}, bf16[8,512,256]{2,1,0:T(8,128)(2,1)}) custom-call(s32[128]{0:T(128)} %order.3, bf16[64,4096]{1,0:T(8,128)(2,1)} %hid.1, f32[1,4096]{1,0:T(1,128)} %bitcast.5, bf16[3,4096,256]{2,1,0:T(8,128)(2,1)} %bitcast.3, f32[256,128]{1,0:T(8,128)} %constant.8.clone.cos_start, f32[256,128]{1,0:T(8,128)} %constant.9.clone.sin_start, ...), custom_call_target="tpu_custom_call" | custom-call | tf_op jit(solution)/shard_map/project/pallas_call | solution.py:215
  53.8 65.0 %attend.1 = bf16[64,4096]{1,0:T(8,128)(2,1)} custom-call(s32[128]{0:T(128)} %order.3, bf16[8,512,128]{2,1,0:T(8,128)(2,1)} %get-tuple-element.7.q_hbm, bf16[4096,256]{1,0:T(8,128)(2,1)} %bitcast.4, bf16[256,4096]{1,0:T(8,128)(2,1)} %w_hbm.1), custom_call_target="tpu_custom_call" | custom-call | tf_op jit(solution)/shard_map/attend/pallas_call | solution.py:491
  118.8 1.9 %copy.11 = bf16[64,4096]{1,0:T(8,128)(2,1)} copy(bf16[64,4096]{1,0:T(8,128)(2,1)} %attend.1) | data formatting | bytes 1048576

commit v5 on v4

--- a/solution.py
+++ b/solution.py
@@ -19,7 +19,6 @@
 ALL = SRC * ROWS
 HALF = HB // 2
 TQ = SRC * HB
-TK = 4096
 MESH = pl.DeviceIdType.MESH
 F32 = jnp.float32
 BF16 = jnp.bfloat16
@@ -73,10 +72,12 @@
     )
 
 
-def project_kernel(
-    order, hid, gain, w_hbm, cos_start, sin_start, cos_row, sin_row, q_out, kv_out,
-    rows, cos, sin, wv, qs, kvs, w_sem, x_send, x_recv, z_send, z_recv,
-    kv_send, kv_recv, q_send, q_recv, own_sem,
+def sublayer_kernel(
+    order, hid, gain, w_hbm, wo_hbm, cos_start, sin_start, cos_row, sin_row, out_ref,
+    rows, cos, sin, wv, qs, kvs, q_ref, kv_ref, w_ref, values, scores_a, scores_b,
+    top_a, top_b, summed, qpos, kpos, o_mine, l_mine, parts, lses, ctx, halves, fulls, mirrored,
+    w_sem, wo_sem, x_send, x_recv, m_send, m_recv, kv_send, kv_recv, q_send, q_recv,
+    o_send, o_recv, l_send, l_recv, h_send, h_recv, f_send, f_recv, z_send, z_recv,
 ):
     y, zl, c, x, zh = place()
     right = device(y, zl, c, (x + 1) % 4, zh)
@@ -90,6 +91,8 @@
     barrier = greet(peers)
     w_copy = pltpu.make_async_copy(w_hbm, wv, w_sem)
     w_copy.start()
+    wo_copy = pltpu.make_async_copy(wo_hbm, w_ref, wo_sem)
+    wo_copy.start()
 
     floats = hid[...].astype(F32)
     scale = lax.rsqrt(jnp.mean(floats * floats, axis=-1, keepdims=True) + 1e-05)
@@ -110,7 +113,7 @@
     def step(p, kind, src, dst, lo, hi, peer):
         return remote(at(src, lo, hi), at(dst, lo, hi), x_send.at[p, kind], x_recv.at[p, kind], peer)
 
-    def ring(p, src, from_left, from_right, far):
+    def spread(p, src, from_left, from_right, far):
         return (
             step(p, 0, src, from_left, 0, HALF, right),
             step(p, 1, src, from_right, HALF, HB, left),
@@ -120,14 +123,14 @@
             step(p, 5, from_right, far, HALF, HB, left),
         )
 
-    mirror_lo = remote(at(OWN, 0, HALF), at(MIR, 0, HALF), z_send.at[0], z_recv.at[0], mirror)
-    mirror_hi = remote(at(OWN, HALF, HB), at(MIR, HALF, HB), z_send.at[1], z_recv.at[1], mirror)
-    near = ring(0, OWN, L0, R0, O0)
-    far = ring(1, MIR, L1, R1, O1)
+    mirror_lo = remote(at(OWN, 0, HALF), at(MIR, 0, HALF), m_send.at[0], m_recv.at[0], mirror)
+    mirror_hi = remote(at(OWN, HALF, HB), at(MIR, HALF, HB), m_send.at[1], m_recv.at[1], mirror)
+    own = spread(0, OWN, L0, R0, O0)
+    mir = spread(1, MIR, L1, R1, O1)
 
     mirror_lo.start()
     mirror_hi.start()
-    for copy in near[:4]:
+    for copy in own[:4]:
         copy.start()
     mine = y * 2 + c
     mine_q = zl * 2 + c
@@ -150,114 +153,46 @@
             kvs[h, lo:hi, HD : 2 * HD] = v[:, lane].astype(BF16)
         for i, (py, pc) in enumerate(kv_peers):
             remote(
-                part(kvs, lo, hi, pc), part(kv_out, lo, hi, mine),
+                part(kvs, lo, hi, pc), part(kv_ref, lo, hi, mine),
                 kv_send.at[i], kv_recv.at[mine], kv_ids[i],
             ).start()
+        kv_ref[mine, lo:hi, :] = kvs[c, lo:hi, :]
+        q_ref[mine_q, lo:hi, :] = qs[c, lo:hi, :]
         for i, (pz, pc) in enumerate(q_peers):
             remote(
-                part(qs, lo, hi, pc), part(q_out, lo, hi, mine_q),
+                part(qs, lo, hi, pc), part(q_ref, lo, hi, mine_q),
                 q_send.at[i], q_recv.at[mine_q], q_ids[i],
             ).start()
 
     w_copy.wait()
     work(OWN, OWN + 1)
-    near[0].wait_recv()
-    near[4].start()
-    near[1].wait_recv()
-    near[5].start()
-    near[2].wait_recv()
-    near[3].wait_recv()
+    own[0].wait_recv()
+    own[4].start()
+    own[1].wait_recv()
+    own[5].start()
+    own[2].wait_recv()
+    own[3].wait_recv()
     work(L0, R0 + 1)
     mirror_lo.wait_recv()
-    far[0].start()
-    far[3].start()
-    near[4].wait_recv()
-    near[5].wait_recv()
+    mir[0].start()
+    mir[3].start()
+    own[4].wait_recv()
+    own[5].wait_recv()
     work(O0, O0 + 1)
     mirror_hi.wait_recv()
-    far[1].start()
-    far[2].start()
+    mir[1].start()
+    mir[2].start()
     work(MIR, MIR + 1)
-    far[0].wait_recv()
-    far[4].start()
-    far[1].wait_recv()
-    far[5].start()
-    far[2].wait_recv()
-    far[3].wait_recv()
+    mir[0].wait_recv()
+    mir[4].start()
+    mir[1].wait_recv()
+    mir[5].start()
+    mir[2].wait_recv()
+    mir[3].wait_recv()
     work(L1, R1 + 1)
-    far[4].wait_recv()
-    far[5].wait_recv()
+    mir[4].wait_recv()
+    mir[5].wait_recv()
     work(O1, O1 + 1)
-    own_kv = pltpu.make_async_copy(kvs.at[c], kv_out.at[mine], own_sem.at[0])
-    own_q = pltpu.make_async_copy(qs.at[c], q_out.at[mine_q], own_sem.at[1])
-    own_kv.start()
-    own_q.start()
-    for copy in (mirror_lo, mirror_hi, *near, *far):
-        copy.wait_send()
-    for i, (py, pc) in enumerate(kv_peers):
-        src = py * 2 + pc
-        done = remote(kvs.at[pc], kv_out.at[src], kv_send.at[i], kv_recv.at[src], kv_ids[i])
-        done.wait_send()
-        done.wait_recv()
-    for i, (pz, pc) in enumerate(q_peers):
-        src = pz * 2 + pc
-        done = remote(qs.at[pc], q_out.at[src], q_send.at[i], q_recv.at[src], q_ids[i])
-        done.wait_send()
-        done.wait_recv()
-    own_kv.wait()
-    own_q.wait()
-
-
-def project(block_order, hidden_in, norm_gain, weight):
-    vmem = pl.BlockSpec(memory_space=pltpu.VMEM)
-    hbm = pl.BlockSpec(memory_space=pl.ANY)
-    dma = pltpu.SemaphoreType.DMA
-    return pl.pallas_call(
-        project_kernel,
-        out_shape=(
-            jax.ShapeDtypeStruct((SRC, ROWS, HD), BF16),
-            jax.ShapeDtypeStruct((SRC, ROWS, 2 * HD), BF16),
-        ),
-        in_specs=[pl.BlockSpec(memory_space=pltpu.SMEM), vmem, vmem, hbm, vmem, vmem, vmem, vmem],
-        out_specs=(hbm, hbm),
-        scratch_shapes=[
-            pltpu.VMEM((ROWS, D), BF16),
-            pltpu.VMEM((ROWS, HD), F32),
-            pltpu.VMEM((ROWS, HD), F32),
-            pltpu.VMEM((3, D, 2 * HD), BF16),
-            pltpu.VMEM((2, ROWS, HD), BF16),
-            pltpu.VMEM((2, ROWS, 2 * HD), BF16),
-            dma, dma((2, 6)), dma((2, 6)), dma((2,)), dma((2,)),
-            dma((SRC,)), dma((SRC,)), dma((SRC,)), dma((SRC,)), dma((2,)),
-        ],
-        compiler_params=pltpu.CompilerParams(
-            collective_id=0, has_side_effects=True, vmem_limit_bytes=60 << 20
-        ),
-        name="project",
-    )(block_order, hidden_in, norm_gain, weight, *tables())
-
-
-def attend_kernel(
-    order, q_hbm, kv_hbm, w_hbm, out_ref,
-    q_ref, kv_ref, w_ref, values, scores_a, scores_b, top_a, top_b, summed, qpos, kpos, o_mine, l_mine, parts, lses,
-    ctx, terms, halves, fulls, mirrored,
-    in_sem, o_send, o_recv, l_send, l_recv, h_send, h_recv, f_send, f_recv, z_send, z_recv,
-):
-    y, zl, c, x, zh = place()
-    right = device(y, zl, c, (x + 1) % 4, zh)
-    left = device(y, zl, c, (x + 3) % 4, zh)
-    mirror = device(y, 3 - zl, c, x, 1 - zh)
-    peers = [((zl + d) % 4, other_core(c, e)) for d, e in OTHERS]
-    ids = [device(y, pz, pc, x, zh) for pz, pc in peers]
-    mine = zl * 2 + c
-    barrier = greet([right, left, mirror] + ids)
-    loads = [
-        pltpu.make_async_copy(src, dst, in_sem.at[i])
-        for i, (src, dst) in enumerate(((q_hbm, q_ref), (kv_hbm, kv_ref), (w_hbm, w_ref)))
-    ]
-    for load in loads:
-        load.start()
-
     lane = lax.broadcasted_iota(jnp.int32, (1, HD), 1)
     row = lax.broadcasted_iota(jnp.int32, (HB, HD), 0)
     for src in range(SRC):
@@ -273,32 +208,39 @@
     diagonal = lax.broadcasted_iota(jnp.int32, (HD, HD), 0) == lax.broadcasted_iota(
         jnp.int32, (HD, HD), 1
     )
-    per = TK // HD
+    per = ALL // HD
     values[:, HD:] = jnp.ones((ALL, HD), BF16)
-    for load in loads:
-        load.wait()
-    values[:, :HD] = kv_ref[:, HD:]
-    pl.semaphore_wait(barrier, len(ids) + 3)
-
-    def score_tile(t, j, scores, top):
+    for copy in (mirror_lo, mirror_hi, *own, *mir):
+        copy.wait_send()
+    wo_copy.wait()
+    for i, (py, pc) in enumerate(kv_peers):
+        src = py * 2 + pc
+        remote(kvs.at[pc], kv_ref.at[src], kv_send.at[i], kv_recv.at[src], kv_ids[i]).wait()
+    for i, (pz, pc) in enumerate(q_peers):
+        src = pz * 2 + pc
+        remote(qs.at[pc], q_ref.at[src], q_send.at[i], q_recv.at[src], q_ids[i]).wait()
+    values[:, :HD] = kv_ref[:, :, HD:].reshape(ALL, HD)
+    peers, ids, mine = q_peers, q_ids, mine_q
+    terms = rows
+
+    def score_chunk(t, scores, top):
         at = pl.ds(pl.multiple_of(t * HB, HB), HB)
         q = q_ref[:, at, :].reshape(TQ, HD)
-        keys = kv_ref[pl.ds(pl.multiple_of(j * TK, TK), TK), 0:HD]
+        keys = kv_ref[:, :, 0:HD].reshape(ALL, HD)
         s = lax.dot_general(q, keys, (((1,), (1,)), ((), ())), preferred_element_type=F32)
         best = top[...]
         for u in range(per):
-            keep = kpos[j * per + u] <= qpos[t]
+            keep = kpos[u] <= qpos[t]
             kept = jnp.where(keep, s[:, u * HD : (u + 1) * HD], -1e30)
-            scores[j * per + u] = kept
+            scores[u] = kept
             best = jnp.maximum(best, kept)
         top[...] = best
 
-    def weigh_tile(j, scores, top):
+    def weigh_chunk(scores, top):
         best = top[...]
-        weight = [jnp.exp2(scores[j * per + u] - best).astype(BF16) for u in range(per)]
-        at = pl.ds(pl.multiple_of(j * TK, TK), TK)
-        summed[...] += jnp.dot(
-            jnp.concatenate(weight, axis=1), values[at, :], preferred_element_type=F32
+        weight = [jnp.exp2(scores[u] - best).astype(BF16) for u in range(per)]
+        summed[...] = jnp.dot(
+            jnp.concatenate(weight, axis=1), values[...], preferred_element_type=F32
         )
 
     def clear(top):
@@ -306,15 +248,10 @@
 
     def attend_chunk(t, scores, top, next_scores=None, next_top=None):
         top[...] = jnp.broadcast_to(jnp.max(top[...], axis=1, keepdims=True), (TQ, HD))
-        summed[...] = jnp.zeros((TQ, 2 * HD), F32)
         if next_top is not None:
             clear(next_top)
-
-        @pl.loop(0, ALL // TK)
-        def _(j):
-            if next_top is not None:
-                score_tile(t + 1, j, next_scores, next_top)
-            weigh_tile(j, scores, top)
+            score_chunk(t + 1, next_scores, next_top)
+        weigh_chunk(scores, top)
 
         total = summed[:, HD:]
         some = total > 0
@@ -324,8 +261,8 @@
         for u in range(SRC // 2):
             block = lse[u * HD : (u + 1) * HD, :]
             line = jnp.sum(jnp.where(diagonal, block, 0.0), axis=0, keepdims=True)
-            l_mine[t, 2 * u, 0:1, :] = line
-            l_mine[t, 2 * u + 1, 0:1, :] = pltpu.roll(line, HB, 1)
+            l_mine[t, 2 * u] = line
+            l_mine[t, 2 * u + 1] = pltpu.roll(line, HB, 1)
         parts[t, mine] = o_mine[t, mine]
         lses[t, mine] = l_mine[t, mine]
         for i, (pz, pc) in enumerate(peers):
@@ -346,16 +283,19 @@
             remote(
                 o_mine.at[t, src], parts.at[t, src], o_send.at[i], o_recv.at[t, src], ids[i]
             ).wait_recv()
-        stats = jnp.concatenate([lses[t, src, 0:1, :] for src in range(SRC)], axis=0)
-        stats = jnp.concatenate([stats] * (HD // SRC), axis=0).T
+        shares = []
         for h in range(2):
-            cols = [stats[0:HB, z * 2 + h : z * 2 + h + 1] for z in range(4)]
-            best = jnp.maximum(jnp.maximum(cols[0], cols[1]), jnp.maximum(cols[2], cols[3]))
-            shares = [jnp.exp2(col - best) for col in cols]
-            total = shares[0] + shares[1] + shares[2] + shares[3]
+            lse = [lses[t, z * 2 + h] for z in range(4)]
+            best = jnp.maximum(jnp.maximum(lse[0], lse[1]), jnp.maximum(lse[2], lse[3]))
+            share = [jnp.exp2(line - best) for line in lse]
+            total = share[0] + share[1] + share[2] + share[3]
+            shares += [line / total for line in share]
+        turned = jnp.concatenate(shares * (HD // SRC), axis=0).T
+        for h in range(2):
             mixed = jnp.zeros((HB, HD), F32)
             for z in range(4):
-                mixed += (shares[z] / total) * parts[t, z * 2 + h].astype(F32)
+                share = turned[0:HB, h * 4 + z : h * 4 + z + 1]
+                mixed += share * parts[t, z * 2 + h].astype(F32)
             ctx[:, h * HD : (h + 1) * HD] = mixed.astype(BF16)
         at = pl.ds(pl.multiple_of(t * HB, HB), HB)
         terms[at, :] = jnp.dot(ctx[...], w_ref[...], preferred_element_type=F32).astype(BF16)
@@ -363,24 +303,24 @@
     def cols(v):
         return pl.ds(v * (D // 2), D // 2)
 
-    def at(slot, lo, v):
+    def cut(slot, lo, v):
         return terms.at[pl.ds(slot * HB + lo, HALF), cols(v)]
 
     def far(p, slot, side, v):
         return remote(
-            at(slot, side * HALF, v), halves.at[p, side, :, cols(v)],
+            cut(slot, side * HALF, v), halves.at[p, side, :, cols(v)],
             h_send.at[p, side, v], h_recv.at[p, side, v], left if side else right,
         )
 
     def near(p, slot, side, upper, v):
         return remote(
-            at(slot, upper * HALF, v), fulls.at[p, side, pl.ds(upper * HALF, HALF), cols(v)],
+            cut(slot, upper * HALF, v), fulls.at[p, side, pl.ds(upper * HALF, HALF), cols(v)],
             f_send.at[p, side, upper, v], f_recv.at[p, side, upper, v], left if side else right,
         )
 
     def over(upper, v):
         return remote(
-            at(MIR, upper * HALF, v), mirrored.at[pl.ds(upper * HALF, HALF), cols(v)],
+            cut(MIR, upper * HALF, v), mirrored.at[pl.ds(upper * HALF, HALF), cols(v)],
             z_send.at[upper, v], z_recv.at[upper, v], mirror,
         )
 
@@ -434,18 +374,21 @@
         def _():
             send_near(1, 0)
 
+        @pl.when(t == MIR + 1)
+        def _():
+            send_over(0)
+
         @pl.when(t == O0 + 1)
         def _():
             send_far(0)
-            send_over(0)
+            send_over(1)
 
         @pl.when(t == L0 + 1)
         def _():
-            send_over(1)
             send_near(0, 1)
 
     clear(top_a)
-    pl.loop(0, ALL // TK)(lambda j: score_tile(0, j, scores_a, top_a))
+    score_chunk(0, scores_a, top_a)
 
     @pl.loop(0, SLOTS // 2 - 1)
     def _(i):
@@ -484,18 +427,25 @@
         remote(o_mine.at[:, src], parts.at[:, src], o_send.at[i], o_recv.at[0, src], ids[i]).wait_send()
 
 
-def attend(block_order, q, kv, out_weight):
+def sublayer(block_order, hidden_in, norm_gain, weight, out_weight):
+    smem = pl.BlockSpec(memory_space=pltpu.SMEM)
     vmem = pl.BlockSpec(memory_space=pltpu.VMEM)
     hbm = pl.BlockSpec(memory_space=pl.ANY)
     dma = pltpu.SemaphoreType.DMA
     return pl.pallas_call(
-        attend_kernel,
+        sublayer_kernel,
         out_shape=jax.ShapeDtypeStruct((HB, D), BF16),
-        in_specs=[pl.BlockSpec(memory_space=pltpu.SMEM), hbm, hbm, hbm],
+        in_specs=[smem, vmem, vmem, hbm, hbm, vmem, vmem, vmem, vmem],
         out_specs=vmem,
         scratch_shapes=[
+            pltpu.VMEM((ROWS, D), BF16),
+            pltpu.VMEM((ROWS, HD), F32),
+            pltpu.VMEM((ROWS, HD), F32),
+            pltpu.VMEM((3, D, 2 * HD), BF16),
+            pltpu.VMEM((2, ROWS, HD), BF16),
+            pltpu.VMEM((2, ROWS, 2 * HD), BF16),
             pltpu.VMEM((SRC, ROWS, HD), BF16),
-            pltpu.VMEM((ALL, 2 * HD), BF16),
+            pltpu.VMEM((SRC, ROWS, 2 * HD), BF16),
             pltpu.VMEM((2 * HD, D), BF16),
             pltpu.VMEM((ALL, 2 * HD), BF16),
             pltpu.VMEM((ALL // HD, TQ, HD), F32),
@@ -506,30 +456,29 @@
             pltpu.VMEM((SLOTS, TQ, HD), jnp.int32),
             pltpu.VMEM((ALL // HD, 1, HD), jnp.int32),
             pltpu.VMEM((SLOTS, SRC, HB, HD), BF16),
-            pltpu.VMEM((SLOTS, SRC, 8, HD), F32),
+            pltpu.VMEM((SLOTS, SRC, 1, HD), F32),
             pltpu.VMEM((SLOTS, SRC, HB, HD), BF16),
-            pltpu.VMEM((SLOTS, SRC, 8, HD), F32),
+            pltpu.VMEM((SLOTS, SRC, 1, HD), F32),
             pltpu.VMEM((HB, 2 * HD), BF16),
-            pltpu.VMEM((ROWS, D), BF16),
             pltpu.VMEM((2, 2, HALF, D), BF16),
             pltpu.VMEM((2, 2, HB, D), BF16),
             pltpu.VMEM((HB, D), BF16),
-            dma((3,)),
+            dma, dma, dma((2, 6)), dma((2, 6)), dma((2,)), dma((2,)),
+            dma((SRC,)), dma((SRC,)), dma((SRC,)), dma((SRC,)),
             dma((SRC,)), dma((SLOTS, SRC)), dma((SRC,)), dma((SLOTS, SRC)),
             dma((2, 2, 2)), dma((2, 2, 2)), dma((2, 2, 2, 2)), dma((2, 2, 2, 2)),
             dma((2, 2)), dma((2, 2)),
         ],
         compiler_params=pltpu.CompilerParams(
-            collective_id=1, has_side_effects=True, vmem_limit_bytes=56 << 20
+            collective_id=0, has_side_effects=True, vmem_limit_bytes=60 << 20
         ),
-        name="attend",
-    )(block_order, q, kv.reshape(ALL, 2 * HD), out_weight)
+        name="sublayer",
+    )(block_order, hidden_in, norm_gain, weight, out_weight, *tables())
 
 
 def local(hidden_in, norm_gain, qkv_weight, out_weight, block_order):
     weight = jnp.transpose(qkv_weight, (1, 0, 2))
-    q, kv = project(block_order, hidden_in, norm_gain[None, :], weight)
-    return attend(block_order, q, kv, out_weight)
+    return sublayer(block_order, hidden_in, norm_gain[None, :], weight, out_weight)
 
 
 def solution(mesh):

time: 123 us -> 120 us (0.976)
  Pallas kernels: 119 us -> 117 us
    pallas_call x2 -> x1, Pallas kernels: 119 us -> 117 us  [sublayer(): pl.pallas_call(sublayer_kernel, out_shape=jax.ShapeDtypeStruct((HB, D), B...]
where the time goes in v5:
time: 120 us; the launch traced here: 119 us
  Pallas kernels  117 us (98%)
  local copies, waits for them, and re-layouts  1.87 us (2%)
    pallas_call x1, Pallas kernels, sublayer(): pl.pallas_call(sublayer_kernel, out_shape=jax.ShapeDtypeStruct((HB, D), B...  117 us

profile of v5, /device:TPU:33, one launch (start us, length us, event | category | flops | bytes accessed | tf_op | source)
XLA Modules:
  0.0 118.7 jit_solution(15428234367887047860)
XLA Ops:
  0.0 116.8 %sublayer.1 = bf16[64,4096]{1,0:T(8,128)(2,1)} custom-call(s32[128]{0:T(128)} %order.1, bf16[64,4096]{1,0:T(8,128)(2,1)} %hid.1, f32[1,4096]{1,0:T(1,128)} %bitcast.3, bf16[3,4096,256]{2,1,0:T(8,128)(2,1)} %bitcast.2, bf16[256,4096]{1,0:T(8,128)(2,1)} %wo_hbm.1, f32[256,128]{1,0:T(8,128)} %constant.8.clone.cos_start, f32[256,128]{1,0:T(8,128)} %constant.9.clone.sin_start, ...), custom_call_target="tpu_custom_call" | custom-call | tf_op jit(solution)/shard_map/sublayer/pallas_call | solution.py:435
  116.8 1.9 %copy.11 = bf16[64,4096]{1,0:T(8,128)(2,1)} copy(bf16[64,4096]{1,0:T(8,128)(2,1)} %sublayer.1) | data formatting | bytes 1048576

commit v6 on v5

--- a/solution.py
+++ b/solution.py
@@ -18,6 +18,8 @@
 SRC = 8
 ALL = SRC * ROWS
 HALF = HB // 2
+CUTS = 4
+WIDTH = D // CUTS
 TQ = SRC * HB
 MESH = pl.DeviceIdType.MESH
 F32 = jnp.float32
@@ -301,7 +303,7 @@
         terms[at, :] = jnp.dot(ctx[...], w_ref[...], preferred_element_type=F32).astype(BF16)
 
     def cols(v):
-        return pl.ds(v * (D // 2), D // 2)
+        return pl.ds(v * WIDTH, WIDTH)
 
     def cut(slot, lo, v):
         return terms.at[pl.ds(slot * HB + lo, HALF), cols(v)]
@@ -327,24 +329,24 @@
     fars, nears = (O0, O1), ((R0, L0), (R1, L1))
 
     def add(lo, v, *more):
-        rows, columns = slice(lo, lo + HALF), slice(v * (D // 2), (v + 1) * (D // 2))
+        rows, columns = slice(lo, lo + HALF), slice(v * WIDTH, (v + 1) * WIDTH)
         total = terms[rows, columns].astype(F32)
         for ref in more:
             total = total + ref[:, columns].astype(F32)
         return total
 
     def store(lo, v, total):
-        terms[lo : lo + HALF, v * (D // 2) : (v + 1) * (D // 2)] = total.astype(BF16)
+        terms[lo : lo + HALF, v * WIDTH : (v + 1) * WIDTH] = total.astype(BF16)
 
     def send_far(p):
-        for v in range(2):
+        for v in range(CUTS):
             for side in range(2):
                 far(p, fars[p], side, v).start()
 
     def send_near(p, side):
         slot = nears[p][side]
         lo = slot * HB + side * HALF
-        for v in range(2):
+        for v in range(CUTS):
             near(p, slot, side, 1 - side, v).start()
             far(p, fars[p], side, v).wait_recv()
             store(lo, v, add(lo, v, halves.at[p, side]))
@@ -359,33 +361,19 @@
             store(lo, v, add(lo, v, fulls.at[1, 0, rows], fulls.at[1, 1, rows]))
             over(upper, v).start()
 
-    def ring(t):
-        pl.when(t > 0)(lambda: term(t - 1))
-
-        @pl.when(t == O1 + 1)
-        def _():
-            send_far(1)
-
-        @pl.when(t == L1 + 1)
-        def _():
-            send_near(1, 1)
-
-        @pl.when(t == R1 + 1)
-        def _():
-            send_near(1, 0)
-
-        @pl.when(t == MIR + 1)
-        def _():
-            send_over(0)
-
-        @pl.when(t == O0 + 1)
-        def _():
-            send_far(0)
-            send_over(1)
-
-        @pl.when(t == L0 + 1)
-        def _():
-            send_near(0, 1)
+    def step_far():
+        term(O1)
+        send_far(1)
+
+    def step_near():
+        term(L1)
+        send_near(1, 1)
+        term(R1)
+        send_near(1, 0)
+
+    def step_mirror():
+        term(MIR)
+        send_over(0)
 
     clear(top_a)
     score_chunk(0, scores_a, top_a)
@@ -393,17 +381,24 @@
     @pl.loop(0, SLOTS // 2 - 1)
     def _(i):
         attend_chunk(2 * i, scores_a, top_a, scores_b, top_b)
-        ring(2 * i)
+        pl.when(i == 1)(step_far)
+        pl.when(i == 2)(step_mirror)
         attend_chunk(2 * i + 1, scores_b, top_b, scores_a, top_a)
-        ring(2 * i + 1)
+        pl.when(i == 1)(step_near)
+        pl.when(i == 2)(lambda: send_over(1))
 
     attend_chunk(SLOTS - 2, scores_a, top_a, scores_b, top_b)
-    ring(SLOTS - 2)
+    term(O0)
+    send_far(0)
+    send_over(2)
+    send_over(3)
     attend_chunk(SLOTS - 1, scores_b, top_b)
+    term(L0)
+    send_near(0, 1)
     term(R0)
     send_near(0, 0)
     term(OWN)
-    for v in range(2):
+    for v in range(CUTS):
         for upper in range(2):
             for side in range(2):
                 near(0, nears[0][side], side, upper, v).wait_recv()
@@ -412,8 +407,8 @@
             total = add(
                 OWN * HB + upper * HALF, v, fulls.at[0, 0, rows], fulls.at[0, 1, rows], mirrored.at[rows]
             )
-            out_ref[rows, v * (D // 2) : (v + 1) * (D // 2)] = total.astype(BF16)
-    for v in range(2):
+            out_ref[rows, v * WIDTH : (v + 1) * WIDTH] = total.astype(BF16)
+    for v in range(CUTS):
         for p in range(2):
             for side in range(2):
                 far(p, fars[p], side, v).wait_send()
@@ -466,8 +461,8 @@
             dma, dma, dma((2, 6)), dma((2, 6)), dma((2,)), dma((2,)),
             dma((SRC,)), dma((SRC,)), dma((SRC,)), dma((SRC,)),
             dma((SRC,)), dma((SLOTS, SRC)), dma((SRC,)), dma((SLOTS, SRC)),
-            dma((2, 2, 2)), dma((2, 2, 2)), dma((2, 2, 2, 2)), dma((2, 2, 2, 2)),
-            dma((2, 2)), dma((2, 2)),
+            dma((2, 2, CUTS)), dma((2, 2, CUTS)), dma((2, 2, 2, CUTS)), dma((2, 2, 2, CUTS)),
+            dma((2, CUTS)), dma((2, CUTS)),
         ],
         compiler_params=pltpu.CompilerParams(
             collective_id=0, has_side_effects=True, vmem_limit_bytes=60 << 20

time: 120 us -> 114 us (0.950)
  the two profiles are of different devices: /device:TPU:33 before, /device:TPU:98 now
where the time goes in v6:
time: 114 us
  Pallas kernels  112 us (98%)
  local copies, waits for them, and re-layouts  1.87 us (2%)
    pallas_call x1, Pallas kernels, sublayer(): pl.pallas_call(sublayer_kernel, out_shape=jax.ShapeDtypeStruct((HB, D), B...  112 us

profile of v6, /device:TPU:98, one launch (start us, length us, event | category | flops | bytes accessed | tf_op | source)
XLA Modules:
  0.0 114.0 jit_solution(14125673709503540496)
XLA Ops:
  0.0 112.1 %sublayer.1 = bf16[64,4096]{1,0:T(8,128)(2,1)} custom-call(s32[128]{0:T(128)} %order.1, bf16[64,4096]{1,0:T(8,128)(2,1)} %hid.1, f32[1,4096]{1,0:T(1,128)} %bitcast.3, bf16[3,4096,256]{2,1,0:T(8,128)(2,1)} %bitcast.2, bf16[256,4096]{1,0:T(8,128)(2,1)} %wo_hbm.1, f32[256,128]{1,0:T(8,128)} %constant.8.clone.cos_start, f32[256,128]{1,0:T(8,128)} %constant.9.clone.sin_start, ...), custom_call_target="tpu_custom_call" | custom-call | tf_op jit(solution)/shard_map/sublayer/pallas_call | solution.py:430
  112.1 1.9 %copy.11 = bf16[64,4096]{1,0:T(8,128)(2,1)} copy(bf16[64,4096]{1,0:T(8,128)(2,1)} %sublayer.1) | data formatting | bytes 1048576

commit v7 on v6

--- a/solution.py
+++ b/solution.py
@@ -99,6 +99,56 @@
     floats = hid[...].astype(F32)
     scale = lax.rsqrt(jnp.mean(floats * floats, axis=-1, keepdims=True) + 1e-05)
     rows[OWN * HB : (OWN + 1) * HB, :] = (floats * scale * gain[...]).astype(BF16)
+    pl.semaphore_wait(barrier, len(peers))
+
+    def piece(slot, upper, v):
+        return rows.at[pl.ds(slot * HB + upper * HALF, HALF), pl.ds(v * (D // 2), D // 2)]
+
+    def spread(p, src, from_left, from_right, far):
+        plan = (
+            (src, from_left, 0, right),
+            (src, from_right, 1, left),
+            (src, from_left, 1, right),
+            (src, from_right, 0, left),
+            (from_left, far, 0, right),
+            (from_right, far, 1, left),
+        )
+        return [
+            [
+                remote(
+                    piece(a, upper, v), piece(b, upper, v),
+                    x_send.at[p, kind, v], x_recv.at[p, kind, v], peer,
+                )
+                for v in range(2)
+            ]
+            for kind, (a, b, upper, peer) in enumerate(plan)
+        ]
+
+    over = [
+        [
+            remote(
+                piece(OWN, upper, v), piece(MIR, upper, v),
+                m_send.at[upper, v], m_recv.at[upper, v], mirror,
+            )
+            for v in range(2)
+        ]
+        for upper in range(2)
+    ]
+    own = spread(0, OWN, L0, R0, O0)
+    mir = spread(1, MIR, L1, R1, O1)
+
+    def arrived(*copies):
+        for pair in copies:
+            for copy in pair:
+                copy.wait_recv()
+
+    for upper in range(2):
+        for copy in over[upper]:
+            copy.start()
+    for kinds in ((0, 1), (2, 3)):
+        for v in range(2):
+            for kind in kinds:
+                own[kind][v].start()
     first_half = lax.broadcasted_iota(jnp.int32, (1, HD), 1) < HD // 2
     for slot in range(SLOTS):
         start = start_of(order, slot, y, zl, c, x, zh) // HB
@@ -107,33 +157,6 @@
         cos[lo:hi, :] = cs * cos_row[...] - sn * sin_row[...]
         sine = sn * cos_row[...] + cs * sin_row[...]
         sin[lo:hi, :] = jnp.where(first_half, -sine, sine)
-    pl.semaphore_wait(barrier, len(peers))
-
-    def at(slot, lo=0, hi=HB):
-        return rows.at[pl.ds(slot * HB + lo, hi - lo), :]
-
-    def step(p, kind, src, dst, lo, hi, peer):
-        return remote(at(src, lo, hi), at(dst, lo, hi), x_send.at[p, kind], x_recv.at[p, kind], peer)
-
-    def spread(p, src, from_left, from_right, far):
-        return (
-            step(p, 0, src, from_left, 0, HALF, right),
-            step(p, 1, src, from_right, HALF, HB, left),
-            step(p, 2, src, from_left, HALF, HB, right),
-            step(p, 3, src, from_right, 0, HALF, left),
-            step(p, 4, from_left, far, 0, HALF, right),
-            step(p, 5, from_right, far, HALF, HB, left),
-        )
-
-    mirror_lo = remote(at(OWN, 0, HALF), at(MIR, 0, HALF), m_send.at[0], m_recv.at[0], mirror)
-    mirror_hi = remote(at(OWN, HALF, HB), at(MIR, HALF, HB), m_send.at[1], m_recv.at[1], mirror)
-    own = spread(0, OWN, L0, R0, O0)
-    mir = spread(1, MIR, L1, R1, O1)
-
-    mirror_lo.start()
-    mirror_hi.start()
-    for copy in own[:4]:
-        copy.start()
     mine = y * 2 + c
     mine_q = zl * 2 + c
 
@@ -159,6 +182,7 @@
                 kv_send.at[i], kv_recv.at[mine], kv_ids[i],
             ).start()
         kv_ref[mine, lo:hi, :] = kvs[c, lo:hi, :]
+        values[pl.ds(pl.multiple_of(mine * ROWS, ROWS) + lo, hi - lo), :HD] = kvs[c, lo:hi, HD:]
         q_ref[mine_q, lo:hi, :] = qs[c, lo:hi, :]
         for i, (pz, pc) in enumerate(q_peers):
             remote(
@@ -168,33 +192,10 @@
 
     w_copy.wait()
     work(OWN, OWN + 1)
-    own[0].wait_recv()
-    own[4].start()
-    own[1].wait_recv()
-    own[5].start()
-    own[2].wait_recv()
-    own[3].wait_recv()
-    work(L0, R0 + 1)
-    mirror_lo.wait_recv()
-    mir[0].start()
-    mir[3].start()
-    own[4].wait_recv()
-    own[5].wait_recv()
-    work(O0, O0 + 1)
-    mirror_hi.wait_recv()
-    mir[1].start()
-    mir[2].start()
-    work(MIR, MIR + 1)
-    mir[0].wait_recv()
-    mir[4].start()
-    mir[1].wait_recv()
-    mir[5].start()
-    mir[2].wait_recv()
-    mir[3].wait_recv()
-    work(L1, R1 + 1)
-    mir[4].wait_recv()
-    mir[5].wait_recv()
-    work(O1, O1 + 1)
+    for v in range(2):
+        for kind in range(2):
+            own[kind][v].wait_recv()
+            own[4 + kind][v].start()
     lane = lax.broadcasted_iota(jnp.int32, (1, HD), 1)
     row = lax.broadcasted_iota(jnp.int32, (HB, HD), 0)
     for src in range(SRC):
@@ -212,16 +213,39 @@
     )
     per = ALL // HD
     values[:, HD:] = jnp.ones((ALL, HD), BF16)
-    for copy in (mirror_lo, mirror_hi, *own, *mir):
-        copy.wait_send()
+    arrived(own[2], own[3])
+    work(L0, R0 + 1)
+    for v in range(2):
+        over[0][v].wait_recv()
+        mir[0][v].start()
+        mir[3][v].start()
+    arrived(own[4], own[5])
+    work(O0, O0 + 1)
+    for v in range(2):
+        over[1][v].wait_recv()
+        mir[1][v].start()
+        mir[2][v].start()
+        mir[0][v].wait_recv()
+        mir[4][v].start()
+    work(MIR, MIR + 1)
+    for v in range(2):
+        mir[1][v].wait_recv()
+        mir[5][v].start()
+    arrived(mir[2], mir[3])
+    work(L1, R1 + 1)
+    arrived(mir[4], mir[5])
+    work(O1, O1 + 1)
+    for pair in (*over, *own, *mir):
+        for copy in pair:
+            copy.wait_send()
     wo_copy.wait()
     for i, (py, pc) in enumerate(kv_peers):
         src = py * 2 + pc
         remote(kvs.at[pc], kv_ref.at[src], kv_send.at[i], kv_recv.at[src], kv_ids[i]).wait()
+        values[pl.ds(pl.multiple_of(src * ROWS, ROWS), ROWS), :HD] = kv_ref[src, :, HD:]
     for i, (pz, pc) in enumerate(q_peers):
         src = pz * 2 + pc
         remote(qs.at[pc], q_ref.at[src], q_send.at[i], q_recv.at[src], q_ids[i]).wait()
-    values[:, :HD] = kv_ref[:, :, HD:].reshape(ALL, HD)
     peers, ids, mine = q_peers, q_ids, mine_q
     terms = rows
 
@@ -320,7 +344,7 @@
             f_send.at[p, side, upper, v], f_recv.at[p, side, upper, v], left if side else right,
         )
 
-    def over(upper, v):
+    def across(upper, v):
         return remote(
             cut(MIR, upper * HALF, v), mirrored.at[pl.ds(upper * HALF, HALF), cols(v)],
             z_send.at[upper, v], z_recv.at[upper, v], mirror,
@@ -359,7 +383,7 @@
             lo = MIR * HB + upper * HALF
             rows = pl.ds(upper * HALF, HALF)
             store(lo, v, add(lo, v, fulls.at[1, 0, rows], fulls.at[1, 1, rows]))
-            over(upper, v).start()
+            across(upper, v).start()
 
     def step_far():
         term(O1)
@@ -402,7 +426,7 @@
         for upper in range(2):
             for side in range(2):
                 near(0, nears[0][side], side, upper, v).wait_recv()
-            over(upper, v).wait_recv()
+            across(upper, v).wait_recv()
             rows = pl.ds(upper * HALF, HALF)
             total = add(
                 OWN * HB + upper * HALF, v, fulls.at[0, 0, rows], fulls.at[0, 1, rows], mirrored.at[rows]
@@ -415,7 +439,7 @@
                 for upper in range(2):
                     near(p, nears[p][side], side, upper, v).wait_send()
         for upper in range(2):
-            over(upper, v).wait_send()
+            across(upper, v).wait_send()
     for i, (pz, pc) in enumerate(peers):
         src = pz * 2 + pc
         remote(l_mine.at[:, src], lses.at[:, src], l_send.at[i], l_recv.at[0, src], ids[i]).wait_send()
@@ -458,7 +482,7 @@
             pltpu.VMEM((2, 2, HALF, D), BF16),
             pltpu.VMEM((2, 2, HB, D), BF16),
             pltpu.VMEM((HB, D), BF16),
-            dma, dma, dma((2, 6)), dma((2, 6)), dma((2,)), dma((2,)),
+            dma, dma, dma((2, 6, 2)), dma((2, 6, 2)), dma((2, 2)), dma((2, 2)),
             dma((SRC,)), dma((SRC,)), dma((SRC,)), dma((SRC,)),
             dma((SRC,)), dma((SLOTS, SRC)), dma((SRC,)), dma((SLOTS, SRC)),
             dma((2, 2, CUTS)), dma((2, 2, CUTS)), dma((2, 2, 2, CUTS)), dma((2, 2, 2, CUTS)),

time: 114 us -> 115 us (level)
  the two profiles are of different devices: /device:TPU:98 before, /device:TPU:33 now
where the time goes in v7:
time: 115 us
  Pallas kernels  113 us (98%)
  local copies, waits for them, and re-layouts  1.87 us (2%)
    pallas_call x1, Pallas kernels, sublayer(): pl.pallas_call(sublayer_kernel, out_shape=jax.ShapeDtypeStruct((HB, D), B...  113 us

profile of v7, /device:TPU:33, one launch (start us, length us, event | category | flops | bytes accessed | tf_op | source)
XLA Modules:
  0.0 115.3 jit_solution(599356446941690753)
XLA Ops:
  0.0 113.4 %sublayer.1 = bf16[64,4096]{1,0:T(8,128)(2,1)} custom-call(s32[128]{0:T(128)} %order.1, bf16[64,4096]{1,0:T(8,128)(2,1)} %hid.1, f32[1,4096]{1,0:T(1,128)} %bitcast.3, bf16[3,4096,256]{2,1,0:T(8,128)(2,1)} %bitcast.2, bf16[256,4096]{1,0:T(8,128)(2,1)} %wo_hbm.1, f32[256,128]{1,0:T(8,128)} %constant.8.clone.cos_start, f32[256,128]{1,0:T(8,128)} %constant.9.clone.sin_start, ...), custom_call_target="tpu_custom_call" | custom-call | tf_op jit(solution)/shard_map/sublayer/pallas_call | solution.py:454
  113.4 1.9 %copy.11 = bf16[64,4096]{1,0:T(8,128)(2,1)} copy(bf16[64,4096]{1,0:T(8,128)(2,1)} %sublayer.1) | data formatting | bytes 1048576

commit v8 on v7

--- a/solution.py
+++ b/solution.py
@@ -75,10 +75,11 @@
 
 
 def sublayer_kernel(
-    order, hid, gain, w_hbm, wo_hbm, cos_start, sin_start, cos_row, sin_row, out_ref,
+    order, hid_hbm, gain_hbm, w_hbm, wo_hbm, cos_start_hbm, sin_start_hbm, cos_row_hbm, sin_row_hbm,
+    out_ref, hid, gain, cos_start, sin_start, cos_row, sin_row,
     rows, cos, sin, wv, qs, kvs, q_ref, kv_ref, w_ref, values, scores_a, scores_b,
     top_a, top_b, summed, qpos, kpos, o_mine, l_mine, parts, lses, ctx, halves, fulls, mirrored,
-    w_sem, wo_sem, x_send, x_recv, m_send, m_recv, kv_send, kv_recv, q_send, q_recv,
+    in_sem, w_sem, wo_sem, x_send, x_recv, m_send, m_recv, kv_send, kv_recv, q_send, q_recv,
     o_send, o_recv, l_send, l_recv, h_send, h_recv, f_send, f_recv, z_send, z_recv,
 ):
     y, zl, c, x, zh = place()
@@ -91,11 +92,22 @@
     q_ids = [device(y, pz, pc, x, zh) for pz, pc in q_peers]
     peers = [right, left, mirror] + kv_ids + q_ids[1:]
     barrier = greet(peers)
+    inputs = [
+        pltpu.make_async_copy(src, dst, in_sem.at[i])
+        for i, (src, dst) in enumerate((
+            (hid_hbm, hid), (gain_hbm, gain), (cos_start_hbm, cos_start),
+            (sin_start_hbm, sin_start), (cos_row_hbm, cos_row), (sin_row_hbm, sin_row),
+        ))
+    ]
+    for copy in inputs:
+        copy.start()
     w_copy = pltpu.make_async_copy(w_hbm, wv, w_sem)
     w_copy.start()
     wo_copy = pltpu.make_async_copy(wo_hbm, w_ref, wo_sem)
     wo_copy.start()
 
+    inputs[0].wait()
+    inputs[1].wait()
     floats = hid[...].astype(F32)
     scale = lax.rsqrt(jnp.mean(floats * floats, axis=-1, keepdims=True) + 1e-05)
     rows[OWN * HB : (OWN + 1) * HB, :] = (floats * scale * gain[...]).astype(BF16)
@@ -149,6 +161,8 @@
         for v in range(2):
             for kind in kinds:
                 own[kind][v].start()
+    for copy in inputs[2:]:
+        copy.wait()
     first_half = lax.broadcasted_iota(jnp.int32, (1, HD), 1) < HD // 2
     for slot in range(SLOTS):
         start = start_of(order, slot, y, zl, c, x, zh) // HB
@@ -167,20 +181,24 @@
         lo, hi = first * HB, last * HB
         chunk = rows[lo:hi, :]
         cs, sn = cos[lo:hi, :], sin[lo:hi, :]
-        q = jnp.dot(chunk, wv[0], preferred_element_type=F32)
+
+        def turn(t):
+            return t * cs + pltpu.roll(t, HD // 2, 1) * sn
+
         k = jnp.dot(chunk, wv[1], preferred_element_type=F32)
         v = jnp.dot(chunk, wv[2], preferred_element_type=F32)
         for h in range(2):
             lane = slice(h * HD, (h + 1) * HD)
-            for out, by, t in ((qs, SCALE, q[:, lane]), (kvs, 1.0, k[:, lane])):
-                turned = t * cs + pltpu.roll(t, HD // 2, 1) * sn
-                out[h, lo:hi, 0:HD] = (turned * by).astype(BF16)
+            kvs[h, lo:hi, 0:HD] = turn(k[:, lane]).astype(BF16)
             kvs[h, lo:hi, HD : 2 * HD] = v[:, lane].astype(BF16)
         for i, (py, pc) in enumerate(kv_peers):
             remote(
                 part(kvs, lo, hi, pc), part(kv_ref, lo, hi, mine),
                 kv_send.at[i], kv_recv.at[mine], kv_ids[i],
             ).start()
+        q = jnp.dot(chunk, wv[0], preferred_element_type=F32)
+        for h in range(2):
+            qs[h, lo:hi, :] = (turn(q[:, h * HD : (h + 1) * HD]) * SCALE).astype(BF16)
         kv_ref[mine, lo:hi, :] = kvs[c, lo:hi, :]
         values[pl.ds(pl.multiple_of(mine * ROWS, ROWS) + lo, hi - lo), :HD] = kvs[c, lo:hi, HD:]
         q_ref[mine_q, lo:hi, :] = qs[c, lo:hi, :]
@@ -454,9 +472,15 @@
     return pl.pallas_call(
         sublayer_kernel,
         out_shape=jax.ShapeDtypeStruct((HB, D), BF16),
-        in_specs=[smem, vmem, vmem, hbm, hbm, vmem, vmem, vmem, vmem],
+        in_specs=[smem] + [hbm] * 8,
         out_specs=vmem,
         scratch_shapes=[
+            pltpu.VMEM((HB, D), BF16),
+            pltpu.VMEM((1, D), F32),
+            pltpu.VMEM((SEQ // HB, HD), F32),
+            pltpu.VMEM((SEQ // HB, HD), F32),
+            pltpu.VMEM((HB, HD), F32),
+            pltpu.VMEM((HB, HD), F32),
             pltpu.VMEM((ROWS, D), BF16),
             pltpu.VMEM((ROWS, HD), F32),
             pltpu.VMEM((ROWS, HD), F32),
@@ -482,7 +506,7 @@
             pltpu.VMEM((2, 2, HALF, D), BF16),
             pltpu.VMEM((2, 2, HB, D), BF16),
             pltpu.VMEM((HB, D), BF16),
-            dma, dma, dma((2, 6, 2)), dma((2, 6, 2)), dma((2, 2)), dma((2, 2)),
+            dma((6,)), dma, dma, dma((2, 6, 2)), dma((2, 6, 2)), dma((2, 2)), dma((2, 2)),
             dma((SRC,)), dma((SRC,)), dma((SRC,)), dma((SRC,)),
             dma((SRC,)), dma((SLOTS, SRC)), dma((SRC,)), dma((SLOTS, SRC)),
             dma((2, 2, CUTS)), dma((2, 2, CUTS)), dma((2, 2, 2, CUTS)), dma((2, 2, 2, CUTS)),

time: 115 us -> 114 us (level)
    pallas_call x1, Pallas kernels: 113 us -> 112 us  [sublayer(): pl.pallas_call(sublayer_kernel, out_shape=jax.ShapeDtypeStruct((HB, D), B...]
where the time goes in v8:
time: 114 us
  Pallas kernels  112 us (98%)
  local copies, waits for them, and re-layouts  1.87 us (2%)
    pallas_call x1, Pallas kernels, sublayer(): pl.pallas_call(sublayer_kernel, out_shape=jax.ShapeDtypeStruct((HB, D), B...  112 us

profile of v8, /device:TPU:33, one launch (start us, length us, event | category | flops | bytes accessed | tf_op | source)
XLA Modules:
  0.0 114.1 jit_solution(4098907880123404316)
XLA Ops:
  0.0 112.2 %sublayer.1 = bf16[64,4096]{1,0:T(8,128)(2,1)} custom-call(s32[128]{0:T(128)} %order.1, bf16[64,4096]{1,0:T(8,128)(2,1)} %hid_hbm.1, f32[1,4096]{1,0:T(1,128)} %bitcast.3, bf16[3,4096,256]{2,1,0:T(8,128)(2,1)} %bitcast.2, bf16[256,4096]{1,0:T(8,128)(2,1)} %wo_hbm.1, f32[256,128]{1,0:T(8,128)} %constant.8.clone.cos_start_hbm, ...), custom_call_target="tpu_custom_call" | custom-call | tf_op jit(solution)/shard_map/sublayer/pallas_call | solution.py:472
  112.3 1.9 %copy.11 = bf16[64,4096]{1,0:T(8,128)(2,1)} copy(bf16[64,4096]{1,0:T(8,128)(2,1)} %sublayer.1) | data formatting | bytes 1048576

commit v9 on v8

--- a/solution.py
+++ b/solution.py
@@ -28,7 +28,7 @@
 O1, L1, R1, MIR, O0, L0, R0, OWN = range(8)
 CHUNKS = ((1, 2), (1, -1), (1, 1), (1, 0), (0, 2), (0, -1), (0, 1), (0, 0))
 SCALE = math.log2(math.e) / HD**0.5
-OTHERS = [(d, e) for d in range(4) for e in range(2)][1:]
+OTHERS = [(0, 1)] + [(d, e) for d in (2, 1, 3) for e in range(2)]
 
 
 def place():
@@ -39,6 +39,12 @@
 
 def device(y, zl, c, x, zh):
     return ((y * 4 + zl) * 2 + c, x * 2 + zh)
+
+
+def far_first(zl):
+    upper = zl // 2
+    turned = zl + upper * (3 - 2 * zl)
+    return [place + upper * (3 - 2 * place) for place in (3, 2, 1 - turned)]
 
 
 def other_core(c, e):
@@ -87,7 +93,7 @@
     left = device(y, zl, c, (x + 3) % 4, zh)
     mirror = device(y, 3 - zl, c, x, 1 - zh)
     kv_peers = [((y + d) % 4, other_core(c, e)) for d, e in OTHERS]
-    q_peers = [((zl + d) % 4, other_core(c, e)) for d, e in OTHERS]
+    q_peers = [(zl, 1 - c)] + [(pz, other_core(c, e)) for pz in far_first(zl) for e in range(2)]
     kv_ids = [device(py, zl, pc, x, zh) for py, pc in kv_peers]
     q_ids = [device(y, pz, pc, x, zh) for pz, pc in q_peers]
     peers = [right, left, mirror] + kv_ids + q_ids[1:]

time: 114 us -> 114 us (level)
  no operation moved by 1% of the time
where the time goes in v9:
time: 114 us
  Pallas kernels  112 us (98%)
  local copies, waits for them, and re-layouts  1.87 us (2%)
    pallas_call x1, Pallas kernels, sublayer(): pl.pallas_call(sublayer_kernel, out_shape=jax.ShapeDtypeStruct((HB, D), B...  112 us

profile of v9, /device:TPU:33, one launch (start us, length us, event | category | flops | bytes accessed | tf_op | source)
XLA Modules:
  0.0 114.3 jit_solution(2420320873582577978)
XLA Ops:
  0.0 112.4 %sublayer.1 = bf16[64,4096]{1,0:T(8,128)(2,1)} custom-call(s32[128]{0:T(128)} %order.1, bf16[64,4096]{1,0:T(8,128)(2,1)} %hid_hbm.1, f32[1,4096]{1,0:T(1,128)} %bitcast.3, bf16[3,4096,256]{2,1,0:T(8,128)(2,1)} %bitcast.2, bf16[256,4096]{1,0:T(8,128)(2,1)} %wo_hbm.1, f32[256,128]{1,0:T(8,128)} %constant.8.clone.cos_start_hbm, ...), custom_call_target="tpu_custom_call" | custom-call | tf_op jit(solution)/shard_map/sublayer/pallas_call | solution.py:478
  112.4 1.9 %copy.11 = bf16[64,4096]{1,0:T(8,128)(2,1)} copy(bf16[64,4096]{1,0:T(8,128)(2,1)} %sublayer.1) | data formatting | bytes 1048576
